TPU v7x, 256 devices: a whole 4x4x8 slice. The times are simulated.
256 devices in a mesh: ctx: 64 (over x, z, y_lo), tp: 4 (over y_hi, core).
Axes of the slice: x: 4, y: 4 (y_hi: 2, y_lo: 2; y = y_hi * 2 + y_lo), z: 8, core: 2. Of those that a mesh axis runs over, the one named last changes fastest.
Arguments:
- queries: bfloat16 [512, 16384], P('ctx', 'tp'), may hold values from -100 to 100
- span_keys: bfloat16 [512, 1024], P('ctx', 'tp'), may hold values from -8 to 8
- span_values: bfloat16 [512, 1024], P('ctx', 'tp'), may hold values from -6 to 6
- cache_keys: bfloat16 [32768, 1024], P('ctx', 'tp'), may hold values from -6 to 6
- cache_values: bfloat16 [32768, 1024], P('ctx', 'tp'), may hold values from -6 to 6
- lengths: int32 [64], P('ctx'), may hold values from 1 to 512, 24576 in all
- start_pos: int32 [1], replicated, may hold values from 12288 to 24576
- w_out: bfloat16 [16384, 16384], P('tp', 'ctx'), may hold values from -3 to 3
Outputs:
- mixed: bfloat16 [512, 16384], P('tp', 'ctx')
Inputs may be any that keep to these rules, and one draw needn't show every extreme that they name: All lengths together sum to 24576.
All inputs are finite; a program needn't handle non-finite values. No bound on the sum of `lengths` on one device may be relied on, other than what follows from the above.
Results may differ from a plain program's by a relative error of at most 0.007.
Values may be sent and summed in bfloat16 or wider, within the bound.
No kernel may reach another device: no remote copies, remote signals or barrier semaphores. Data moves between devices by JAX's collectives and lax.ppermute only.
A program may use at most 128 MiB of HBM per device.

v0:
```python
import math

import jax
import jax.numpy as jnp
from jax import lax
from jax.sharding import PartitionSpec as P

HEADS = 128
KV_HEADS = 8
HEAD_DIM = 128


very_low = -1e30


def prefix(x, axis, combine, identity):
    devices, place = (lax.axis_size(axis), lax.axis_index(axis))
    everything = lax.all_gather(x, axis)
    start = jnp.broadcast_to(jnp.asarray(identity, x.dtype), x.shape)

    def hop(k, before):
        reached = k < place
        new = combine(before, everything[k])
        return jnp.where(reached, new, before)

    return lax.fori_loop(0, devices, hop, start)


def partial_block(query_block, key_rows, value_rows, visible_mask):
    scores = jnp.einsum("rkge,cke->rkgc", query_block, key_rows, preferred_element_type=jnp.float32)
    scores = scores * (1.0 / math.sqrt(HEAD_DIM))
    mask_full = visible_mask[:, None, None, :]
    masked = jnp.where(mask_full, scores, very_low)
    part_max = jnp.max(masked, axis=-1)
    exp_terms = jnp.where(mask_full, jnp.exp(masked - part_max[..., None]), 0.0)
    part_sum = jnp.sum(exp_terms, axis=-1)
    weights = exp_terms.astype(jnp.bfloat16)
    summed = jnp.einsum("rkgc,cke->rkge", weights, value_rows, preferred_element_type=jnp.float32)
    part_out = (summed / jnp.maximum(part_sum, 1.0)[..., None]).astype(jnp.bfloat16)
    return (part_out, part_max, part_sum)


def absorb(running, part):
    top_score, numerator, denominator = running
    part_out, part_max, part_sum = part
    new_top = jnp.maximum(top_score, part_max)
    rescale = jnp.exp(top_score - new_top)
    share_now = part_sum * jnp.exp(part_max - new_top)
    numerator = numerator * rescale[..., None] + share_now[..., None] * part_out.astype(jnp.float32)
    denominator = denominator * rescale + share_now
    return (new_top, numerator, denominator)


def add_ints(earlier, later):
    return earlier + later


def shards(queries, span_keys, span_values, cache_keys, cache_values, lengths, start_pos, w_out):
    tok_rows = queries.shape[0]
    kv_local = span_keys.shape[1] // HEAD_DIM
    group_size = HEADS // KV_HEADS
    own_queries = queries.reshape(tok_rows, kv_local, group_size, HEAD_DIM)
    offset = prefix(lengths, "ctx", add_ints, jnp.zeros_like(lengths))
    visible_count = jnp.clip(start_pos - offset, 0, lengths)
    span_k, span_v = (
        lax.all_gather(span_keys, "ctx", axis=0, tiled=True),
        lax.all_gather(span_values, "ctx", axis=0, tiled=True),
    )
    all_rows = span_k.shape[0]
    first_token = lax.axis_index("ctx") * tok_rows
    own_positions = first_token + jnp.arange(tok_rows, dtype=jnp.int32)
    causal = jnp.arange(all_rows, dtype=jnp.int32)[None, :] <= own_positions[:, None]
    running = (
        jnp.full((tok_rows, kv_local, group_size), very_low, jnp.float32),
        jnp.zeros((tok_rows, kv_local, group_size, HEAD_DIM), jnp.float32),
        jnp.zeros((tok_rows, kv_local, group_size), jnp.float32),
    )
    running = absorb(
        running,
        partial_block(
            own_queries,
            span_k.reshape(all_rows, kv_local, HEAD_DIM),
            span_v.reshape(all_rows, kv_local, HEAD_DIM),
            causal,
        ),
    )
    cache_rows = cache_keys.shape[0]
    gathered = lax.all_gather(queries, "ctx", axis=0, tiled=True)
    total_queries = gathered.shape[0]
    block_rows = 128
    query_blocks = gathered.reshape(
        total_queries // block_rows, block_rows, kv_local, group_size, HEAD_DIM
    )
    key_rows = cache_keys.reshape(cache_rows, kv_local, HEAD_DIM)
    value_rows = cache_values.reshape(cache_rows, kv_local, HEAD_DIM)
    visible_mask = (jnp.arange(cache_rows, dtype=jnp.int32) < visible_count[0])[None, :]

    def attend_block(query_block):
        return partial_block(query_block, key_rows, value_rows, visible_mask)

    part_outs, part_maxes, part_sums = lax.map(attend_block, query_blocks)
    shard_total = lax.axis_size("ctx")
    part_outs = part_outs.reshape(shard_total, tok_rows, kv_local * group_size * HEAD_DIM)
    part_maxes = part_maxes.reshape(shard_total, tok_rows, kv_local * group_size)
    part_sums = part_sums.reshape(shard_total, tok_rows, kv_local * group_size)
    part_outs, part_maxes, part_sums = (
        lax.all_to_all(
            part_outs.astype(jnp.float32), "ctx", split_axis=0, concat_axis=0, tiled=True
        ).astype(part_outs.dtype),
        lax.all_to_all(part_maxes, "ctx", split_axis=0, concat_axis=0, tiled=True),
        lax.all_to_all(part_sums, "ctx", split_axis=0, concat_axis=0, tiled=True),
    )

    def absorb_one(carried, shard_item):
        one_out, one_max, one_sum = shard_item
        merged = absorb(
            carried,
            (
                one_out.reshape(tok_rows, kv_local, group_size, HEAD_DIM),
                one_max.reshape(tok_rows, kv_local, group_size),
                one_sum.reshape(tok_rows, kv_local, group_size),
            ),
        )
        return (merged, None)

    running, _ = lax.scan(absorb_one, running, (part_outs, part_maxes, part_sums))
    top_score, numerator, denominator = running
    attention = (
        (numerator / denominator[..., None])
        .astype(jnp.bfloat16)
        .reshape(tok_rows, kv_local * group_size * HEAD_DIM)
    )
    projected = jnp.dot(
        lax.all_gather(attention, "ctx", axis=0, tiled=True),
        w_out,
        preferred_element_type=jnp.float32,
    )
    return lax.psum_scatter(projected, "tp", scatter_dimension=0, tiled=True).astype(jnp.bfloat16)


def solution(mesh):
    return jax.shard_map(
        shards,
        mesh=mesh,
        in_specs=(
            P("ctx", "tp"),
            P("ctx", "tp"),
            P("ctx", "tp"),
            P("ctx", "tp"),
            P("ctx", "tp"),
            P("ctx"),
            P(),
            P("tp", "ctx"),
        ),
        out_specs=P("tp", "ctx"),
        check_vma=False,
    )
```

profile of v0, /device:TPU:2, one launch (start us, length us, event | category | flops | bytes accessed | tf_op | source)
XLA Modules:
  0.0 1185.4 jit_solution(2091920467629998302)
XLA Ops:
  10.6 24.9 %all-reduce = s32[64]{0:T(128)S(1)} all-reduce(s32[64]{0:T(128)S(1)} %dynamic-update-slice), channel_id=2, replica_groups=mesh['ctx'=64,'tp'=4] {'ctx'}, use_global_device_ids=true, to_apply=%add | all-reduce | flops 64 | bytes 512
  35.5 80.9 %while.42 = (s32[]{:T(128)}, s32[1]{0:T(128)}, s32[]{:T(128)}, s32[64,1]{0,1:T(1,128)S(1)}, s32[]{:T(128)}) while((s32[]{:T(128)}, s32[1]{0:T(128)}, s32[]{:T(128)}, s32[64,1]{0,1:T(1,128)S(1)}, s32[]{:T(128)}) %tuple.99), condition=%wide.region_3.4_spmd, body=%wide.region_2.3_spmd.sunk | while | flops 5 | bytes 107 | solution.py:26
  119.0 175.1 %all-gather.4.cloned.1.call-done = bf16[512,4096]{1,0:T(8,128)(2,1)} async-done(((bf16[8,4096]{1,0:T(8,128)(2,1)}), bf16[512,4096]{1,0:T(8,128)(2,1)}) %all-gather.4.cloned.1.call-update) | async-done | bytes 4194320 | tf_op jit(solution)/shard_map/all_gather | solution.py:88
  294.1 5.4 copy.59
  299.5 37.2 %while.44 = (s32[]{:T(128)}, bf16[4,128,2,16,128]{4,1,3,2,0:T(8,128)(2,1)}, f32[4,128,2,16]{1,3,2,0:T(8,128)S(1)}, f32[4,128,2,16]{1,3,2,0:T(8,128)S(1)}, bf16[4...) while((s32[]{:T(128)}, ...), condition=%wide.region_7.8_spmd.clone, body=%wide.region_4.7_spmd.clone.sunk | while | flops 1102049792 | bytes 30067816 | solution.py:101
  302.6 2.4 fusion.53
  305.1 3.8 fusion.54
  311.9 2.4 fusion.53
  314.3 3.8 fusion.54
  321.2 2.4 fusion.53
  323.6 3.8 fusion.54
  332.9 3.8 fusion.54
  338.1 29.2 %all-to-all-start = ((f32[64,1,256]{2,1,0:T(1,128)}), f32[64,1,256]{2,1,0:T(1,128)S(1)}, u32[]{:S(2)}, u32[]{:S(2)}) async-start(f32[64,1,256]{2,1,0:T(1,128)} %reshape.111), calls=%async_computation | async-start | bytes 131072 | tf_op jit(solution)/shard_map/all_to_all | solution.py:110
  368.7 9.0 all-to-all-done
  377.6 6.8 all-to-all-start.1
  384.5 6.8 copy.45
  391.3 7.3 reshape.100
  398.6 11.6 all-to-all-start.2
  410.3 174.5 %all_gather.18 = bf16[512,256]{1,0:T(8,128)(2,1)S(1)} all-gather(bf16[8,256]{1,0:T(8,128)(2,1)S(1)} %copy-done.2), channel_id=1, replica_groups=mesh['ctx'=64,'tp'=4] {'ctx'}, dimensions={0}, use_global_device_ids=true | all-gather | bytes 266240 | tf_op jit(solution)/shard_map/all_gather | solution.py:66
  584.9 145.0 %all_gather.19 = bf16[512,256]{1,0:T(8,128)(2,1)S(1)} all-gather(bf16[8,256]{1,0:T(8,128)(2,1)S(1)} %copy-done.3), channel_id=1, replica_groups=mesh['ctx'=64,'tp'=4] {'ctx'}, dimensions={0}, use_global_device_ids=true | all-gather | bytes 266240 | tf_op jit(solution)/shard_map/all_gather | solution.py:67
  733.4 81.1 %while.43 = (s32[]{:T(128)}, f32[8,2,16]{2,1,0:T(2,128)S(1)}, f32[8,2,16,128]{3,2,1,0:T(8,128)S(1)}, f32[8,2,16]{2,1,0:T(2,128)S(1)}, f32[64,8,32]{2,1,0:T(8,128...) while((s32[]{:T(128)}, f32[8,2,16]{2,1,0:T(2,128)S(1)}, ...), condition=%wide.region_9.10_spmd, body=%wide.region_8.9_spmd.sunk | while | flops 132610 | bytes 870493 | solution.py:126
  815.4 304.5 %all-gather.6.cloned.1.call-done = bf16[512,4096]{1,0:T(8,128)(2,1)} async-done(((bf16[8,4096]{1,0:T(8,128)(2,1)}), bf16[512,4096]{1,0:T(8,128)(2,1)}) %all-gather.6.cloned.1.call-update) | async-done | bytes 4194320 | tf_op jit(solution)/shard_map/all_gather | solution.py:134
  1119.9 4.3 fusion.42
  1124.2 53.1 %reduce-scatter.2.cloned.1.call-done = f32[128,256]{1,0:T(8,128)} async-done(((f32[512,256]{1,0:T(8,128)}), f32[128,256]{1,0:T(8,128)}) %reduce-scatter.2.cloned.1.call-update) | async-done | bytes 131088 | tf_op jit(solution)/shard_map/reduce_scatter | solution.py:138
  (584 shorter events, 146.0 us)
Async XLA Ops:
  6.5 1113.4 %copy-start = (bf16[4096,256]{1,0:T(8,128)(2,1)S(1)}, bf16[4096,256]{1,0:T(8,128)(2,1)}, u32[]{:S(2)}) copy-start(bf16[4096,256]{1,0:T(8,128)(2,1)} %param.21) | copy-start | bytes 6291460
  6.5 287.6 %all-gather.4.cloned.1.call-start = ((), (), s32[]{:S(2)}) async-start(), calls=%async_computation.4 | async-start | bytes 4259840 | tf_op jit(solution)/shard_map/all_gather | solution.py:88
  338.1 39.5 %all-to-all-start = ((f32[64,1,256]{2,1,0:T(1,128)}), f32[64,1,256]{2,1,0:T(1,128)S(1)}, u32[]{:S(2)}, u32[]{:S(2)}) async-start(f32[64,1,256]{2,1,0:T(1,128)} %reshape.111), calls=%async_computation | async-start | bytes 131072 | tf_op jit(solution)/shard_map/all_to_all | solution.py:110
  377.6 21.0 %all-to-all-start.1 = ((f32[64,1,256]{2,1,0:T(1,128)}), f32[64,1,256]{2,1,0:T(1,128)S(1)}, u32[]{:S(2)}, u32[]{:S(2)}) async-start(f32[64,1,256]{2,1,0:T(1,128)} %reshape.113), calls=%async_computation.1 | async-start | bytes 131072 | tf_op jit(solution)/shard_map/all_to_all | solution.py:111
  398.6 11.6 copy-start.2
  398.6 186.3 %copy-start.3 = (bf16[8,256]{1,0:T(8,128)(2,1)S(1)}, bf16[8,256]{1,0:T(8,128)(2,1)}, u32[]{:S(2)}) copy-start(bf16[8,256]{1,0:T(8,128)(2,1)} %param.16) | copy-start | bytes 12292
  398.6 331.5 %copy-start.1 = (bf16[8,4096]{1,0:T(8,128)(2,1)S(1)}, bf16[8,4096]{1,0:T(8,128)(2,1)}, u32[]{:S(2)}) copy-start(bf16[8,4096]{1,0:T(8,128)(2,1)} %param.14) | copy-start | bytes 196612
  398.6 334.8 %all-to-all-start.2 = ((bf16[64,8,4096]{2,1,0:T(8,128)(2,1)}), bf16[64,8,4096]{2,1,0:T(8,128)(2,1)}, u32[]{:S(2)}, u32[]{:S(2)}) async-start(bf16[64,8,4096]{2,1,0:T(8,128)(2,1)} %reshape.100), calls=%async_computation.2 | async-start | bytes 8388608 | tf_op jit(solution)/shard_map/all_to_all | solution.py:107
  410.2 709.7 %all-gather.6.cloned.1.call-start = ((), (), s32[]{:S(2)}) async-start(), calls=%async_computation.5 | async-start | bytes 4259840 | tf_op jit(solution)/shard_map/all_gather | solution.py:134
  815.3 362.0 %reduce-scatter.2.cloned.1.call-start = ((), (), s32[]{:S(2)}) async-start(), calls=%async_computation.6 | async-start | bytes 655360 | tf_op jit(solution)/shard_map/reduce_scatter | solution.py:138
Sparse Core Ops, SparseCore 0:
  9.1 284.9 all-gather.3
  815.5 304.4 all-gather.5
  1124.3 52.9 reduce-scatter.1
where the time goes:
time: 1190 us
  waiting for transfers between devices  543 us (46%)
  blocking collectives  344 us (29%)
  local copies, waits for them, and re-layouts  85 us (7%)
  other arithmetic  79.5 us (7%)
  starting transfers between devices  47.6 us (4%)
  loops' own time  44.9 us (4%)
  matrix products  26.9 us (2%)
  between operations  14.7 us (1%)
    all_gather x1, waiting for transfers between devices, shards(): lax.all_gather(attention, 'ctx', axis=0, tiled=True)  305 us
    all_gather x1, waiting for transfers between devices, shards(): gathered = lax.all_gather(queries, 'ctx', axis=0, tiled=True)  175 us
    all_gather x1, blocking collectives, shards(): lax.all_gather(span_keys, 'ctx', axis=0, tiled=True)  174 us
    all_gather x1, blocking collectives, shards(): lax.all_gather(span_values, 'ctx', axis=0, tiled=True)  145 us
    while x64, other arithmetic  54.8 us
    reduce_scatter x1, waiting for transfers between devices, shards(): lax.psum_scatter(projected, 'tp', scatter_dimension=0, tiled=True)  53.1 us
    another operation x1, loops' own time, prefix(): return lax.fori_loop(0, devices, hop, start)  42.1 us
    dynamic_slice x64, local copies, waits for them, and re-layouts, hop(): new = combine(before, everything[k])  38.8 us
  transfers between devices with their start and end apart: 6, of which 4 were waited for; matrix products, arithmetic and copies ran while one was open for 5% of the time, Pallas kernels for 0%

commit v1 on v0

v1 whole, which is shorter than its diff:
```python
import functools
import math

import jax
import jax.numpy as jnp
from jax import lax
from jax.experimental import pallas as pl
from jax.experimental.pallas import tpu as pltpu
from jax.sharding import Mesh, PartitionSpec as P

HEADS = 128
KV_HEADS = 8
HEAD_DIM = 128
GROUP = HEADS // KV_HEADS
HIDE = -1e30
SCALE = 1.0 / math.sqrt(HEAD_DIM)
LOG2E = 1.4426950408889634

X, Z, YL, YH, CORE = 4, 8, 2, 2, 2
ZY = Z * YL
CTX_AXES = ("x", "z", "yl")
TP_AXES = ("yh", "c")
ZY_AXES = ("z", "yl")
TOK = 8
ROWS = 512
SPAN = 16
GTOK = ZY * TOK
KV_LOCAL = 2
HEADS_LOCAL = KV_LOCAL * GROUP
WIDTH = HEADS_LOCAL * HEAD_DIM
CACHE = X * ROWS
COLS = CACHE + 128


def attend_kernel(info, q_ref, kv0, kv1, kv2, kv3, out_ref, keys, values, seen):
    lane = lax.broadcasted_iota(jnp.int32, (ROWS, 128), 1)
    row = lax.broadcasted_iota(jnp.int32, (ROWS, 128), 0)
    for k, kv in enumerate((kv0, kv1, kv2, kv3)):
        bias = jnp.where((lane == 0) & (row >= info[k]), HIDE, 0.0).astype(jnp.bfloat16)
        for g in range(KV_LOCAL):
            at = pl.ds(k * ROWS, ROWS)
            keys[g, at, 0:128] = kv[0:ROWS, g * 128 : (g + 1) * 128]
            keys[g, at, 128:256] = bias
            values[g, at, 0:128] = kv[0:ROWS, 256 + g * 128 : 256 + (g + 1) * 128]
            at = pl.ds(CACHE + k * SPAN, SPAN)
            keys[g, at, 0:128] = kv[ROWS : ROWS + SPAN, g * 128 : (g + 1) * 128]
            values[g, at, 0:128] = kv[ROWS : ROWS + SPAN, 256 + g * 128 : 256 + (g + 1) * 128]
    lane = lax.broadcasted_iota(jnp.int32, (128, 128), 1)
    row = lax.broadcasted_iota(jnp.int32, (128, 128), 0)
    marks = jnp.where((row < 64) & (lane == 64 + row), 1.0, 0.0) + jnp.where(
        (row >= 64) & (lane == 0), HIDE, 0.0
    )
    marks = marks.astype(jnp.bfloat16)
    for g in range(KV_LOCAL):
        keys[g, pl.ds(CACHE, 128), 128:256] = marks
        keys[g, pl.ds(CACHE + 64, 64), 0:128] = jnp.zeros((64, 128), jnp.bfloat16)
        values[g, pl.ds(CACHE + 64, 64), 0:128] = jnp.zeros((64, 128), jnp.bfloat16)
        values[g, :, 128:256] = jnp.ones((COLS, 128), jnp.bfloat16)
    slot = lane - 64
    part, inner = slot // SPAN, slot % SPAN
    first = jnp.where(
        part == 0, info[4], jnp.where(part == 1, info[5], jnp.where(part == 2, info[6], info[7]))
    )
    hidden = (inner >= TOK) | (first + inner > info[8] + row)
    extra = jnp.where(lane == 0, 1.0, jnp.where((slot >= 0) & hidden, HIDE, 0.0))
    seen[...] = extra.astype(jnp.bfloat16)

    def one_group(g):
        def body(step, stats):
            for j in range(4):
                h = g * GROUP + step * 4 + j
                at = pl.ds(pl.multiple_of(h * 128, 128), 128)
                query = jnp.concatenate([q_ref[:, at], seen[...]], axis=1)
                scores = lax.dot_general(
                    query, keys[g], (((1,), (1,)), ((), ())), preferred_element_type=jnp.float32
                )
                top = jnp.max(scores, axis=1, keepdims=True)
                weights = jnp.exp2((scores - top) * (SCALE * LOG2E)).astype(jnp.bfloat16)
                both = jnp.dot(weights, values[g], preferred_element_type=jnp.float32)
                total = both[:, 128:256]
                out_ref[:, at] = (both[:, 0:128] / total).astype(jnp.bfloat16)
                stats = jnp.where(lane % HEADS_LOCAL == h, top * SCALE + jnp.log(total), stats)
            return stats

        return body

    stats = jnp.zeros((GTOK, 128), jnp.float32)
    for g in range(KV_LOCAL):
        stats = lax.fori_loop(0, GROUP // 4, one_group(g), stats)
    high = stats.astype(jnp.bfloat16).astype(jnp.float32)
    rest = stats - high
    middle = rest.astype(jnp.bfloat16).astype(jnp.float32)
    low = rest - middle
    pieces = jnp.where(lane < 32, high, jnp.where(lane < 64, middle, low))
    out_ref[:, WIDTH : WIDTH + 128] = pieces.astype(jnp.bfloat16)


def attend(info, queries, parts):
    vmem = pl.BlockSpec(memory_space=pltpu.VMEM)
    return pl.pallas_call(
        attend_kernel,
        out_shape=jax.ShapeDtypeStruct((GTOK, WIDTH + 128), jnp.bfloat16),
        in_specs=[pl.BlockSpec(memory_space=pltpu.SMEM)] + [vmem] * 5,
        out_specs=vmem,
        scratch_shapes=[
            pltpu.VMEM((KV_LOCAL, COLS, 256), jnp.bfloat16),
            pltpu.VMEM((KV_LOCAL, COLS, 256), jnp.bfloat16),
            pltpu.VMEM((GTOK, 128), jnp.bfloat16),
        ],
        compiler_params=pltpu.CompilerParams(vmem_limit_bytes=32 << 20),
        cost_estimate=pl.CostEstimate(
            flops=8 * HEADS_LOCAL * GTOK * COLS * 128,
            bytes_accessed=4 << 20,
            transcendentals=HEADS_LOCAL * GTOK * COLS,
        ),
        name="attend",
    )(info, queries, *parts)


def merge_kernel(got, out_ref):
    pieces = got[:, :, WIDTH : WIDTH + 128].astype(jnp.float32)
    lse = pieces + (pltpu.roll(pieces, 96, 2) + pltpu.roll(pieces, 64, 2))
    share = jnp.exp(lse - jnp.max(lse, axis=0, keepdims=True))
    share = share / jnp.sum(share, axis=0, keepdims=True)
    for h in range(HEADS_LOCAL):
        at = slice(h * 128, (h + 1) * 128)
        merged = jnp.sum(share[:, :, h : h + 1] * got[:, :, at].astype(jnp.float32), axis=0)
        out_ref[:, :, at] = jnp.broadcast_to(merged.astype(jnp.bfloat16)[None], (ZY, TOK, 128))


def merge(got):
    vmem = pl.BlockSpec(memory_space=pltpu.VMEM)
    return pl.pallas_call(
        merge_kernel,
        out_shape=jax.ShapeDtypeStruct((ZY, TOK, WIDTH), jnp.bfloat16),
        in_specs=[vmem],
        out_specs=vmem,
        compiler_params=pltpu.CompilerParams(vmem_limit_bytes=16 << 20),
        cost_estimate=pl.CostEstimate(flops=2 << 20, bytes_accessed=2 << 20, transcendentals=4096),
        name="merge",
    )(got)


def along_x(v, k):
    return lax.ppermute(v, "x", [((i + k) % X, i) for i in range(X)])


def shards(queries, span_keys, span_values, cache_keys, cache_values, lengths, start_pos, w_out):
    x, zy = lax.axis_index("x"), lax.axis_index(ZY_AXES)
    tp = lax.axis_index(TP_AXES)
    spread = jnp.broadcast_to(queries[None], (ZY, TOK, WIDTH))
    gathered = lax.all_to_all(spread, ZY_AXES, 0, 0, tiled=True).reshape(GTOK, WIDTH)
    own = jnp.concatenate(
        [
            jnp.concatenate([cache_keys, span_keys, jnp.zeros_like(span_keys)], axis=0),
            jnp.concatenate([cache_values, span_values, jnp.zeros_like(span_values)], axis=0),
        ],
        axis=1,
    )
    parts = [own] + [along_x(own, k) for k in (1, 3, 2)]
    order = jnp.array([0, 1, 3, 2], jnp.int32)
    sizes = lax.all_to_all(
        jnp.broadcast_to(lengths[None], (X * ZY, 1)), CTX_AXES, 0, 0, tiled=True
    ).reshape(1, X * ZY)
    shard = ((x + order) % X) * ZY + zy
    index = jnp.arange(X * ZY, dtype=jnp.int32)[None]
    offset = jnp.sum(jnp.where(index < shard[:, None], sizes, 0), axis=1)
    filled = jnp.sum(jnp.where(index == shard[:, None], sizes, 0), axis=1)
    limit = jnp.clip(start_pos - offset, 0, filled)
    info = jnp.concatenate([limit, shard * TOK, (x * GTOK)[None]]).astype(jnp.int32)

    partial = attend(info, gathered, parts)

    w_held, _ = lax.optimization_barrier((w_out, parts[3]))
    weights = [w_out, along_x(w_held, 1), along_x(w_held, 2), along_x(w_held, 3)]

    got = lax.all_to_all(partial.reshape(ZY, TOK, WIDTH + 128), ZY_AXES, 0, 0, tiled=True)
    merged = lax.all_to_all(merge(got), ZY_AXES, 0, 0, tiled=True).reshape(GTOK, WIDTH)

    projected = jnp.stack(
        [
            jnp.dot(merged, w, preferred_element_type=jnp.float32).astype(jnp.bfloat16)
            for w in weights
        ]
    )
    total = None
    for r in range(X):
        block = lax.dynamic_index_in_dim(projected, (tp + r - x) % X, 0, keepdims=False)
        pairs = [(a * 4 + b, ((b + r) % X) * 4 + a) for a in range(X) for b in range(4)]
        term = lax.ppermute(block, ("x", "yh", "c"), pairs).astype(jnp.float32)
        total = term if total is None else total + term
    return total.astype(jnp.bfloat16)


def solution(mesh):
    fine = Mesh(mesh.devices.reshape(X, Z, YL, YH, CORE), CTX_AXES + TP_AXES)
    split = P(CTX_AXES, TP_AXES)
    return jax.shard_map(
        shards,
        mesh=fine,
        in_specs=(split, split, split, split, split, P(CTX_AXES), P(), P(TP_AXES, CTX_AXES)),
        out_specs=P(TP_AXES, CTX_AXES),
        check_vma=False,
    )
```

time: 1190 us -> 236 us (0.20)
  waiting for transfers between devices: 543 us -> 110 us
  blocking collectives: 344 us -> 57.3 us
  local copies, waits for them, and re-layouts: 85 us -> 2.01 us
  other arithmetic: 79.5 us -> 2.24 us
  loops' own time: 44.9 us -> 0 us
  Pallas kernels: 0 us -> 27.9 us
  starting transfers between devices: 47.6 us -> 25.9 us
  matrix products: 26.9 us -> 6.54 us
  between operations: 14.7 us -> 1.55 us
    all_gather x2 -> x0, waiting for transfers between devices: 480 us -> none  [the longest x1 305 us: shards(): lax.all_gather(attention, 'ctx', axis=0, tiled=True)]
    all_gather x2 -> x0, blocking collectives: 319 us -> none  [the longest x1 174 us: shards(): lax.all_gather(span_keys, 'ctx', axis=0, tiled=True)]
    ppermute x0 -> x10, waiting for transfers between devices: none -> 85.3 us  [the longest x6 82.1 us: along_x(): return lax.ppermute(v, 'x', [((i + k) % X, i) for i in range(X)])]
    all_to_all x0 -> x2, blocking collectives: none -> 57.3 us  [the longest x1 35.1 us: shards(): lax.all_to_all(partial.reshape(ZY, TOK, WIDTH + 128), ZY_AXES, 0, 0, tile...]
    while x64 -> x0, other arithmetic: 54.8 us -> none
    reduce_scatter x1 -> x0, waiting for transfers between devices: 53.1 us -> none  [shards(): lax.psum_scatter(projected, 'tp', scatter_dimension=0, tiled=True)]
    another operation x3 -> x0, loops' own time: 44.9 us -> none  [the longest x1 42.1 us: prefix(): return lax.fori_loop(0, devices, hop, start)]
    dynamic_slice x132 -> x0, local copies, waits for them, and re-layouts: 44.8 us -> none  [the longest x64 38.8 us: hop(): new = combine(before, everything[k])]
  transfers between devices with their start and end apart: 6 -> 12, of which waited for: 4 -> 7; matrix products, arithmetic and copies ran while one was open for 5% -> 3% of each run, Pallas kernels for 0% -> 0%
where the time goes in v1:
time: 236 us; the launch traced here: 233 us
  waiting for transfers between devices  110 us (47%)
  blocking collectives  57.3 us (24%)
  Pallas kernels  27.9 us (12%)
  starting transfers between devices  25.9 us (11%)
  matrix products  6.54 us (3%)
    ppermute x6, waiting for transfers between devices, along_x(): return lax.ppermute(v, 'x', [((i + k) % X, i) for i in range(X)])  82.1 us
    all_to_all x1, blocking collectives, shards(): lax.all_to_all(partial.reshape(ZY, TOK, WIDTH + 128), ZY_AXES, 0, 0, tile...  35.1 us
    pallas_call x1, Pallas kernels, attend(): pl.pallas_call(attend_kernel, out_shape=jax.ShapeDtypeStruct((GTOK, WIDTH...  26 us
    all_to_all x1, blocking collectives, shards(): lax.all_to_all(jnp.broadcast_to(lengths[None], (X * ZY, 1)), CTX_AXES, 0,...  22.3 us
    all_to_all x1, waiting for transfers between devices, shards(): lax.all_to_all(merge(got), ZY_AXES, 0, 0, tiled=True).reshape(GTOK, WIDTH)  22.2 us
    ppermute x4, starting transfers between devices, shards(): term = lax.ppermute(block, ('x', 'yh', 'c'), pairs).astype(jnp.float32)  10.1 us
    ppermute x6, starting transfers between devices, along_x(): return lax.ppermute(v, 'x', [((i + k) % X, i) for i in range(X)])  8.46 us
    dot_general x4, matrix products, shards(): jnp.dot(merged, w, preferred_element_type=jnp.float32).astype(jnp.bfloat16)  6.54 us
  transfers between devices with their start and end apart: 12, of which 7 were waited for; matrix products, arithmetic and copies ran while one was open for 3% of the time, Pallas kernels for 0%

profile of v1, /device:TPU:2, one launch (start us, length us, event | category | flops | bytes accessed | tf_op | source)
XLA Modules:
  0.0 233.1 jit_solution(11623116388710584477)
XLA Ops:
  0.8 22.3 %all_to_all.21 = s32[64,1,1]{2,1,0:T(1,128)S(1)} all-to-all(s32[64,1,1]{2,1,0:T(1,128)S(1)} %broadcast_in_dim.39), channel_id=1, replica_groups=mesh['x'=4,'z'=8,'yl'=2,'yh'=2,'c'=2] {'x','z','yl'}, dimensions={0} | all-to-all | bytes 512 | tf_op jit(solution)/shard_map/all_to_all | solution.py:162
  23.0 1.9 broadcast_in_dim.44
  25.0 3.7 %all-to-all-start.1 = ((bf16[16,8,4096]{2,1,0:T(8,128)(2,1)}), bf16[16,8,4096]{2,1,0:T(8,128)(2,1)S(1)}, u32[]{:S(2)}, u32[]{:S(2)}) async-start(bf16[16,8,4096]{2,1,0:T(8,128)(2,1)} %broadcast_in_dim.44), calls=%async_computation.1 | async-start | bytes 2097152 | tf_op jit(solution)/shard_map/all_to_all | solution.py:152
  28.7 1.3 collective-permute-start.2
  30.1 1.5 collective-permute-start
  34.3 11.3 %collective-permute-done.2.kv3 = bf16[528,512]{1,0:T(8,128)(2,1)S(1)} collective-permute-done((bf16[528,512]{1,0:T(8,128)(2,1)S(1)}, bf16[528,512]{1,0:T(8,128)(2,1)S(1)}, u32[]{:S(2)}, u32[]{:S(2)}) %collective-permute-start.2) | collective-permute-done | bytes 540704 | tf_op jit(solution)/shard_map/ppermute | solution.py:145
  45.5 8.4 %collective-permute-done.kv1 = bf16[528,512]{1,0:T(8,128)(2,1)S(1)} collective-permute-done((bf16[528,512]{1,0:T(8,128)(2,1)S(1)}, bf16[528,512]{1,0:T(8,128)(2,1)S(1)}, u32[]{:S(2)}, u32[]{:S(2)}) %collective-permute-start) | collective-permute-done | bytes 540704 | tf_op jit(solution)/shard_map/ppermute | solution.py:145
  54.0 2.3 all-to-all-done.1
  56.3 26.0 %attend.1 = bf16[128,4224]{1,0:T(8,128)(2,1)S(1)} custom-call(s32[9]{0:T(128)S(1)} %pad_add_fusion.info, bf16[128,4096]{1,0:T(8,128)(2,1)S(1)} %bitcast.37, bf16[528,512]{1,0:T(8,128)(2,1)S(1)} %maximum_maximum_fusion.kv0, bf16[528,512]{1,0:T(8,128)(2,1)S(1)} %collective-permute-done.kv1, bf16[528,512]{1,0:T(8,128)(2,1)S(1)} %collective-permute-done.1.kv2, ...), custom_call_target="tpu_custom_call" | custom-call | flops 9126805504 | bytes 4194304 | tf_op jit(solution)/shard_map/attend/pallas_call | solution.py:100
  82.2 35.1 %all_to_all.22.got = bf16[16,8,4224]{2,1,0:T(8,128)(2,1)S(1)} all-to-all(bf16[16,8,4224]{2,1,0:T(8,128)(2,1)S(1)} %bitcast.36), channel_id=1, replica_groups=mesh['x'=4,'z'=8,'yl'=2,'yh'=2,'c'=2] {'z','yl'}, dimensions={0} | all-to-all | bytes 2162688 | tf_op jit(solution)/shard_map/all_to_all | solution.py:177
  117.3 1.9 merge.1
  119.2 3.7 %all-to-all-start.3 = ((bf16[16,8,4096]{2,1,0:T(8,128)(2,1)}), bf16[16,8,4096]{2,1,0:T(8,128)(2,1)S(1)}, u32[]{:S(2)}, u32[]{:S(2)}) async-start(bf16[16,8,4096]{2,1,0:T(8,128)(2,1)} %merge.1), calls=%async_computation.3 | async-start | bytes 2097152 | tf_op jit(solution)/shard_map/all_to_all | solution.py:178
  122.8 2.5 %collective-permute-start.3 = (bf16[4096,256]{1,0:T(8,128)(2,1)S(1)}, bf16[4096,256]{1,0:T(8,128)(2,1)}, u32[]{:S(2)}, u32[]{:S(2)}) collective-permute-start(bf16[4096,256]{1,0:T(8,128)(2,1)S(1)} %copy-done), channel_id=1, source_target_pairs={{64,0},{128,64},{192,128},{0,192},{65,1},{129,65},{193,129},{1,193... | collective-permute-start | bytes 6291464 | tf_op jit(solution)/shard_map/ppermute | solution.py:145
  126.2 1.7 collective-permute-start.5
  127.9 22.2 %all-to-all-done.3 = bf16[16,8,4096]{2,1,0:T(8,128)(2,1)S(1)} async-done(((bf16[16,8,4096]{2,1,0:T(8,128)(2,1)}), bf16[16,8,4096]{2,1,0:T(8,128)(2,1)S(1)}, u32[]{:S(2)}, u32[]{:S(2)}) %all-to-all-start.3) | async-done | bytes 1048608 | tf_op jit(solution)/shard_map/all_to_all | solution.py:178
  150.5 20.9 %collective-permute-done.3 = bf16[4096,256]{1,0:T(8,128)(2,1)} collective-permute-done((bf16[4096,256]{1,0:T(8,128)(2,1)S(1)}, bf16[4096,256]{1,0:T(8,128)(2,1)}, u32[]{:S(2)}, u32[]{:S(2)}) %collective-permute-start.3) | collective-permute-done | bytes 2097184 | tf_op jit(solution)/shard_map/ppermute | solution.py:145
  171.5 2.0 fusion.1
  173.5 41.4 %collective-permute-done.4 = bf16[4096,256]{1,0:T(8,128)(2,1)} collective-permute-done((bf16[4096,256]{1,0:T(8,128)(2,1)S(1)}, bf16[4096,256]{1,0:T(8,128)(2,1)}, u32[]{:S(2)}, u32[]{:S(2)}) %collective-permute-start.4) | collective-permute-done | bytes 2097184 | tf_op jit(solution)/shard_map/ppermute | solution.py:145
  214.9 2.0 fusion.2
  217.0 2.0 fusion.3
  219.1 3.0 %collective-permute-start.6 = (bf16[128,256]{1,0:T(8,128)(2,1)S(1)}, bf16[128,256]{1,0:T(8,128)(2,1)S(1)}, u32[]{:S(2)}, u32[]{:S(2)}) collective-permute-start(bf16[128,256]{1,0:T(8,128)(2,1)S(1)} %get-tuple-element.11), channel_id=1, source_target_pairs={{0,0},{1,64},{2,128},{3,192},{64,1},{65,65},{66,129},{67,193},{128... | collective-permute-start | bytes 196616 | tf_op jit(solution)/shard_map/ppermute | solution.py:190
  222.2 3.1 %collective-permute-start.8 = (bf16[128,256]{1,0:T(8,128)(2,1)S(1)}, bf16[128,256]{1,0:T(8,128)(2,1)S(1)}, u32[]{:S(2)}, u32[]{:S(2)}) collective-permute-start(bf16[128,256]{1,0:T(8,128)(2,1)S(1)} %get-tuple-element.13), channel_id=1, source_target_pairs={{0,128},{1,192},{2,0},{3,64},{64,129},{65,193},{66,1},{67,65},{128... | collective-permute-start | bytes 196616 | tf_op jit(solution)/shard_map/ppermute | solution.py:190
  225.3 3.9 %collective-permute-start.9 = (bf16[128,256]{1,0:T(8,128)(2,1)S(1)}, bf16[128,256]{1,0:T(8,128)(2,1)S(1)}, u32[]{:S(2)}, u32[]{:S(2)}) collective-permute-start(bf16[128,256]{1,0:T(8,128)(2,1)S(1)} %get-tuple-element.12), channel_id=1, source_target_pairs={{0,192},{1,0},{2,64},{3,128},{64,193},{65,1},{66,65},{67,129},{128... | collective-permute-start | bytes 196616 | tf_op jit(solution)/shard_map/ppermute | solution.py:190
  229.2 3.2 %collective-permute-done.9 = bf16[128,256]{1,0:T(8,128)(2,1)S(1)} collective-permute-done((bf16[128,256]{1,0:T(8,128)(2,1)S(1)}, bf16[128,256]{1,0:T(8,128)(2,1)S(1)}, u32[]{:S(2)}, u32[]{:S(2)}) %collective-permute-start.9) | collective-permute-done | bytes 65568 | tf_op jit(solution)/shard_map/ppermute | solution.py:190
  (32 shorter events, 4.2 us)
Async XLA Ops:
  0.0 28.7 %copy-start.4 = (bf16[8,256]{1,0:T(8,128)(2,1)S(1)}, bf16[8,256]{1,0:T(8,128)(2,1)}, u32[]{:S(2)}) copy-start(bf16[8,256]{1,0:T(8,128)(2,1)} %param.10) | copy-start | bytes 12292
  0.0 28.7 %copy-start.3 = (bf16[8,256]{1,0:T(8,128)(2,1)S(1)}, bf16[8,256]{1,0:T(8,128)(2,1)}, u32[]{:S(2)}) copy-start(bf16[8,256]{1,0:T(8,128)(2,1)} %param.11) | copy-start | bytes 12292
  0.0 28.7 %copy-start.2 = (bf16[512,256]{1,0:T(8,128)(2,1)S(1)}, bf16[512,256]{1,0:T(8,128)(2,1)}, u32[]{:S(2)}) copy-start(bf16[512,256]{1,0:T(8,128)(2,1)} %param.12) | copy-start | bytes 786436
  0.0 28.7 %copy-start.1 = (bf16[512,256]{1,0:T(8,128)(2,1)S(1)}, bf16[512,256]{1,0:T(8,128)(2,1)}, u32[]{:S(2)}) copy-start(bf16[512,256]{1,0:T(8,128)(2,1)} %param.13) | copy-start | bytes 786436
  23.0 9.1 %copy-start.5 = (s32[4]{0:T(128)S(1)}, s32[4]{0:T(128)}, u32[]{:S(2)}) copy-start(s32[4]{0:T(128)} %constant.78.clone) | copy-start | bytes 52
  25.0 31.3 %all-to-all-start.1 = ((bf16[16,8,4096]{2,1,0:T(8,128)(2,1)}), bf16[16,8,4096]{2,1,0:T(8,128)(2,1)S(1)}, u32[]{:S(2)}, u32[]{:S(2)}) async-start(bf16[16,8,4096]{2,1,0:T(8,128)(2,1)} %broadcast_in_dim.44), calls=%async_computation.1 | async-start | bytes 2097152 | tf_op jit(solution)/shard_map/all_to_all | solution.py:152
  28.7 16.8 %collective-permute-start.2 = (bf16[528,512]{1,0:T(8,128)(2,1)S(1)}, bf16[528,512]{1,0:T(8,128)(2,1)S(1)}, u32[]{:S(2)}, u32[]{:S(2)}) collective-permute-start(bf16[528,512]{1,0:T(8,128)(2,1)S(1)} %maximum_maximum_fusion.kv0), channel_id=1, source_target_pairs={{128,0},{192,64},{0,128},{64,192},{129,1},{193,65},{1,129},{65,193... | collective-permute-start | bytes 1622024 | tf_op jit(solution)/shard_map/ppermute | solution.py:145
  30.1 23.9 %collective-permute-start = (bf16[528,512]{1,0:T(8,128)(2,1)S(1)}, bf16[528,512]{1,0:T(8,128)(2,1)S(1)}, u32[]{:S(2)}, u32[]{:S(2)}) collective-permute-start(bf16[528,512]{1,0:T(8,128)(2,1)S(1)} %maximum_maximum_fusion.kv0), channel_id=1, source_target_pairs={{64,0},{128,64},{192,128},{0,192},{65,1},{129,65},{193,129},{1,193... | collective-permute-start | bytes 1622024 | tf_op jit(solution)/shard_map/ppermute | solution.py:145
  31.6 22.4 %collective-permute-start.1 = (bf16[528,512]{1,0:T(8,128)(2,1)S(1)}, bf16[528,512]{1,0:T(8,128)(2,1)S(1)}, u32[]{:S(2)}, u32[]{:S(2)}) collective-permute-start(bf16[528,512]{1,0:T(8,128)(2,1)S(1)} %maximum_maximum_fusion.kv0), channel_id=1, source_target_pairs={{192,0},{0,64},{64,128},{128,192},{193,1},{1,65},{65,129},{129,193... | collective-permute-start | bytes 1622024 | tf_op jit(solution)/shard_map/ppermute | solution.py:145
  117.3 5.5 %copy-start = (bf16[4096,256]{1,0:T(8,128)(2,1)S(1)}, bf16[4096,256]{1,0:T(8,128)(2,1)}, u32[]{:S(2)}) copy-start(bf16[4096,256]{1,0:T(8,128)(2,1)} %param.16) | copy-start | bytes 6291460
  119.2 30.9 %all-to-all-start.3 = ((bf16[16,8,4096]{2,1,0:T(8,128)(2,1)}), bf16[16,8,4096]{2,1,0:T(8,128)(2,1)S(1)}, u32[]{:S(2)}, u32[]{:S(2)}) async-start(bf16[16,8,4096]{2,1,0:T(8,128)(2,1)} %merge.1), calls=%async_computation.3 | async-start | bytes 2097152 | tf_op jit(solution)/shard_map/all_to_all | solution.py:178
  122.8 48.6 %collective-permute-start.3 = (bf16[4096,256]{1,0:T(8,128)(2,1)S(1)}, bf16[4096,256]{1,0:T(8,128)(2,1)}, u32[]{:S(2)}, u32[]{:S(2)}) collective-permute-start(bf16[4096,256]{1,0:T(8,128)(2,1)S(1)} %copy-done), channel_id=1, source_target_pairs={{64,0},{128,64},{192,128},{0,192},{65,1},{129,65},{193,129},{1,193... | collective-permute-start | bytes 6291464 | tf_op jit(solution)/shard_map/ppermute | solution.py:145
  125.4 89.5 %collective-permute-start.4 = (bf16[4096,256]{1,0:T(8,128)(2,1)S(1)}, bf16[4096,256]{1,0:T(8,128)(2,1)}, u32[]{:S(2)}, u32[]{:S(2)}) collective-permute-start(bf16[4096,256]{1,0:T(8,128)(2,1)S(1)} %copy-done), channel_id=1, source_target_pairs={{128,0},{192,64},{0,128},{64,192},{129,1},{193,65},{1,129},{65,193... | collective-permute-start | bytes 6291464 | tf_op jit(solution)/shard_map/ppermute | solution.py:145
  126.2 90.8 %collective-permute-start.5 = (bf16[4096,256]{1,0:T(8,128)(2,1)S(1)}, bf16[4096,256]{1,0:T(8,128)(2,1)}, u32[]{:S(2)}, u32[]{:S(2)}) collective-permute-start(bf16[4096,256]{1,0:T(8,128)(2,1)S(1)} %copy-done), channel_id=1, source_target_pairs={{192,0},{0,64},{64,128},{128,192},{193,1},{1,65},{65,129},{129,193... | collective-permute-start | bytes 6291464 | tf_op jit(solution)/shard_map/ppermute | solution.py:145
  219.1 10.1 %collective-permute-start.6 = (bf16[128,256]{1,0:T(8,128)(2,1)S(1)}, bf16[128,256]{1,0:T(8,128)(2,1)S(1)}, u32[]{:S(2)}, u32[]{:S(2)}) collective-permute-start(bf16[128,256]{1,0:T(8,128)(2,1)S(1)} %get-tuple-element.11), channel_id=1, source_target_pairs={{0,0},{1,64},{2,128},{3,192},{64,1},{65,65},{66,129},{67,193},{128... | collective-permute-start | bytes 196616 | tf_op jit(solution)/shard_map/ppermute | solution.py:190
  222.1 7.1 %collective-permute-start.7 = (bf16[128,256]{1,0:T(8,128)(2,1)S(1)}, bf16[128,256]{1,0:T(8,128)(2,1)S(1)}, u32[]{:S(2)}, u32[]{:S(2)}) collective-permute-start(bf16[128,256]{1,0:T(8,128)(2,1)S(1)} %get-tuple-element.14), channel_id=1, source_target_pairs={{0,64},{1,128},{2,192},{3,0},{64,65},{65,129},{66,193},{67,1},{128... | collective-permute-start | bytes 196616 | tf_op jit(solution)/shard_map/ppermute | solution.py:190
  222.2 7.0 %collective-permute-start.8 = (bf16[128,256]{1,0:T(8,128)(2,1)S(1)}, bf16[128,256]{1,0:T(8,128)(2,1)S(1)}, u32[]{:S(2)}, u32[]{:S(2)}) collective-permute-start(bf16[128,256]{1,0:T(8,128)(2,1)S(1)} %get-tuple-element.13), channel_id=1, source_target_pairs={{0,128},{1,192},{2,0},{3,64},{64,129},{65,193},{66,1},{67,65},{128... | collective-permute-start | bytes 196616 | tf_op jit(solution)/shard_map/ppermute | solution.py:190
  225.3 7.1 %collective-permute-start.9 = (bf16[128,256]{1,0:T(8,128)(2,1)S(1)}, bf16[128,256]{1,0:T(8,128)(2,1)S(1)}, u32[]{:S(2)}, u32[]{:S(2)}) collective-permute-start(bf16[128,256]{1,0:T(8,128)(2,1)S(1)} %get-tuple-element.12), channel_id=1, source_target_pairs={{0,192},{1,0},{2,64},{3,128},{64,193},{65,1},{66,65},{67,129},{128... | collective-permute-start | bytes 196616 | tf_op jit(solution)/shard_map/ppermute | solution.py:190

commit v2 on v1

v2 whole, which is shorter than its diff:
```python
import math

import jax
import jax.numpy as jnp
from jax import lax
from jax.experimental import pallas as pl
from jax.experimental.pallas import tpu as pltpu
from jax.sharding import Mesh, PartitionSpec as P

HEADS = 128
KV_HEADS = 8
HEAD_DIM = 128
GROUP = HEADS // KV_HEADS
HIDE = -1e30
SCALE = 1.0 / math.sqrt(HEAD_DIM)
LOG2E = 1.4426950408889634

X, ZQ, ZP, YL, YH, CORE = 4, 4, 2, 2, 2, 2
MEMBERS = 16
CTX_AXES = ("x", "zq", "zp", "yl")
TP_AXES = ("yh", "c")
NEAR_AXES = ("x", "zp", "yl")
COLUMN_AXES = ("zq", "zp", "yl")
TOK = 8
ROWS = 512
SPAN = 16
GTOK = MEMBERS * TOK
KV_LOCAL = 2
HEADS_LOCAL = KV_LOCAL * GROUP
WIDTH = HEADS_LOCAL * HEAD_DIM
PARTS = ZQ
CACHE = PARTS * ROWS
COLS = CACHE + 128
STEPS = (0, 1, 3, 2)


def step_of(k):
    return jnp.where(k == 2, 3, jnp.where(k == 3, 2, k))


def pack_kernel(queries, size0, size1, size2, size3, out_ref):
    lane = lax.broadcasted_iota(jnp.int32, (TOK, 128), 1)
    tail = jnp.zeros((TOK, 128), jnp.float32)
    for k, size in enumerate((size0, size1, size2, size3)):
        high = size[0] // 256
        low = size[0] - high * 256
        tail = jnp.where(lane == k, high.astype(jnp.float32), tail)
        tail = jnp.where(lane == PARTS + k, low.astype(jnp.float32), tail)
    out_ref[:, :, 0:WIDTH] = jnp.broadcast_to(queries[...][None], (MEMBERS, TOK, WIDTH))
    out_ref[:, :, WIDTH : WIDTH + 128] = jnp.broadcast_to(
        tail.astype(jnp.bfloat16)[None], (MEMBERS, TOK, 128)
    )


def pack(queries, sizes):
    vmem = pl.BlockSpec(memory_space=pltpu.VMEM)
    smem = pl.BlockSpec(memory_space=pltpu.SMEM)
    return pl.pallas_call(
        pack_kernel,
        out_shape=jax.ShapeDtypeStruct((MEMBERS, TOK, WIDTH + 128), jnp.bfloat16),
        in_specs=[vmem] + [smem] * PARTS,
        out_specs=vmem,
        compiler_params=pltpu.CompilerParams(vmem_limit_bytes=16 << 20),
        cost_estimate=pl.CostEstimate(flops=1 << 19, bytes_accessed=1 << 20, transcendentals=0),
        name="pack",
    )(queries, *sizes)


def visible_rows(info, tail):
    lane = lax.broadcasted_iota(jnp.int32, (GTOK, 128), 1)
    row = lax.broadcasted_iota(jnp.int32, (GTOK, 128), 0)
    source = row // TOK
    held = (row % TOK == 0) & (lane < 2 * PARTS)
    size = jnp.where(held, tail * jnp.where(lane < PARTS, 256.0, 1.0), 0.0)
    place = (info[2] + step_of(lane % PARTS)) % ZQ
    shard = (source // 4) * 16 + place * 4 + source % 4
    start = info[0].astype(jnp.float32)
    out = []
    for k in range(PARTS):
        own = info[1] * 16 + ((info[2] + STEPS[k]) % ZQ) * 4 + info[3]
        offset = jnp.sum(jnp.where(shard < own, size, 0.0), keepdims=True)
        filled = jnp.sum(jnp.where(shard == own, size, 0.0), keepdims=True)
        out.append(jnp.clip(start - offset, 0.0, filled))
    return out


def attend_kernel(info, q_ref, *refs):
    kvs, (out_ref, keys, values, seen) = refs[: 2 * PARTS], refs[2 * PARTS :]
    limits = visible_rows(info, q_ref[:, WIDTH : WIDTH + 128].astype(jnp.float32))
    lane = lax.broadcasted_iota(jnp.int32, (ROWS, 128), 1)
    row = lax.broadcasted_iota(jnp.int32, (ROWS, 128), 0).astype(jnp.float32)
    for k in range(PARTS):
        bias = jnp.where((lane == 0) & (row >= limits[k]), HIDE, 0.0).astype(jnp.bfloat16)
        for g in range(KV_LOCAL):
            kv = kvs[g * PARTS + k]
            at = pl.ds(k * ROWS, ROWS)
            keys[g, at, 0:128] = kv[0:ROWS, 0:128]
            keys[g, at, 128:256] = bias
            values[g, at, 0:128] = kv[0:ROWS, 128:256]
            at = pl.ds(CACHE + k * SPAN, SPAN)
            keys[g, at, 0:128] = kv[ROWS : ROWS + SPAN, 0:128]
            values[g, at, 0:128] = kv[ROWS : ROWS + SPAN, 128:256]
    lane = lax.broadcasted_iota(jnp.int32, (128, 128), 1)
    row = lax.broadcasted_iota(jnp.int32, (128, 128), 0)
    marks = jnp.where((row < 64) & (lane == 64 + row), 1.0, 0.0) + jnp.where(
        (row >= 64) & (lane == 0), HIDE, 0.0
    )
    for g in range(KV_LOCAL):
        keys[g, pl.ds(CACHE, 128), 128:256] = marks.astype(jnp.bfloat16)
        keys[g, pl.ds(CACHE + 64, 64), 0:128] = jnp.zeros((64, 128), jnp.bfloat16)
        values[g, pl.ds(CACHE + 64, 64), 0:128] = jnp.zeros((64, 128), jnp.bfloat16)
        values[g, :, 128:256] = jnp.ones((COLS, 128), jnp.bfloat16)
    slot = lane - 64
    part, inner = slot // SPAN, slot % SPAN
    shard = info[1] * 16 + ((info[2] + step_of(part)) % ZQ) * 4 + info[3]
    source = row // TOK
    chunk = (source // 4) * 16 + info[2] * 4 + source % 4
    hidden = (inner >= TOK) | (shard * TOK + inner > chunk * TOK + row % TOK)
    extra = jnp.where(lane == 0, 1.0, jnp.where((slot >= 0) & hidden, HIDE, 0.0))
    seen[...] = extra.astype(jnp.bfloat16)

    per = 2
    mask = jnp.concatenate([seen[...]] * per, axis=0)

    def one_group(g, stats):
        def columns(h):
            return pl.ds(pl.multiple_of((g * GROUP + h) * 128, 128), 128)

        def score(i):
            heads = [q_ref[:, columns(i * per + j)] for j in range(per)]
            query = jnp.concatenate([jnp.concatenate(heads, axis=0), mask], axis=1)
            return lax.dot_general(
                query, keys[g], (((1,), (1,)), ((), ())), preferred_element_type=jnp.float32
            )

        scores = score(0)
        for i in range(GROUP // per):
            later = score(i + 1) if i + 1 < GROUP // per else None
            top = jnp.max(scores, axis=1, keepdims=True)
            weights = jnp.exp2((scores - top) * (SCALE * LOG2E)).astype(jnp.bfloat16)
            both = jnp.dot(weights, values[g], preferred_element_type=jnp.float32)
            total = both[:, 128:256]
            outs = (both[:, 0:128] / total).astype(jnp.bfloat16)
            lse = top * SCALE + jnp.log(total)
            for j in range(per):
                h = i * per + j
                out_ref[:, columns(h)] = outs[j * GTOK : (j + 1) * GTOK]
                mine = lane % HEADS_LOCAL == g * GROUP + h
                stats = jnp.where(mine, lse[j * GTOK : (j + 1) * GTOK], stats)
            scores = later
        return stats

    stats = lax.fori_loop(0, KV_LOCAL, one_group, jnp.zeros((GTOK, 128), jnp.float32))
    high = stats.astype(jnp.bfloat16).astype(jnp.float32)
    rest = stats - high
    middle = rest.astype(jnp.bfloat16).astype(jnp.float32)
    low = rest - middle
    pieces = jnp.where(lane < HEADS_LOCAL, high, jnp.where(lane < 2 * HEADS_LOCAL, middle, low))
    out_ref[:, WIDTH : WIDTH + 128] = pieces.astype(jnp.bfloat16)


def attend(info, queries, parts):
    vmem = pl.BlockSpec(memory_space=pltpu.VMEM)
    return pl.pallas_call(
        attend_kernel,
        out_shape=jax.ShapeDtypeStruct((GTOK, WIDTH + 128), jnp.bfloat16),
        in_specs=[pl.BlockSpec(memory_space=pltpu.SMEM)] + [vmem] * (1 + 2 * PARTS),
        out_specs=vmem,
        scratch_shapes=[
            pltpu.VMEM((KV_LOCAL, COLS, 256), jnp.bfloat16),
            pltpu.VMEM((KV_LOCAL, COLS, 256), jnp.bfloat16),
            pltpu.VMEM((GTOK, 128), jnp.bfloat16),
        ],
        compiler_params=pltpu.CompilerParams(vmem_limit_bytes=32 << 20),
        cost_estimate=pl.CostEstimate(
            flops=8 * HEADS_LOCAL * GTOK * COLS * 128,
            bytes_accessed=4 << 20,
            transcendentals=HEADS_LOCAL * GTOK * COLS,
        ),
        name="attend",
    )(info, queries, *parts)


def merge_kernel(got, out_ref):
    pieces = got[:, :, WIDTH : WIDTH + 128].astype(jnp.float32)
    lse = pieces + (pltpu.roll(pieces, 96, 2) + pltpu.roll(pieces, 64, 2))
    share = jnp.exp(lse - jnp.max(lse, axis=0, keepdims=True))
    share = share / jnp.sum(share, axis=0, keepdims=True)
    for h in range(HEADS_LOCAL):
        at = slice(h * 128, (h + 1) * 128)
        merged = jnp.sum(share[:, :, h : h + 1] * got[:, :, at].astype(jnp.float32), axis=0)
        out_ref[:, :, at] = jnp.broadcast_to(merged.astype(jnp.bfloat16)[None], (MEMBERS, TOK, 128))


def merge(got):
    vmem = pl.BlockSpec(memory_space=pltpu.VMEM)
    return pl.pallas_call(
        merge_kernel,
        out_shape=jax.ShapeDtypeStruct((MEMBERS, TOK, WIDTH), jnp.bfloat16),
        in_specs=[vmem],
        out_specs=vmem,
        compiler_params=pltpu.CompilerParams(vmem_limit_bytes=16 << 20),
        cost_estimate=pl.CostEstimate(flops=2 << 20, bytes_accessed=2 << 20, transcendentals=4096),
        name="merge",
    )(got)


def along(v, axis, k):
    return lax.ppermute(v, axis, [((i + k) % 4, i) for i in range(4)])


def after(v, *earlier):
    return lax.optimization_barrier((v, *earlier))[0]


def shards(queries, span_keys, span_values, cache_keys, cache_values, lengths, start_pos, w_out):
    x, zq, near = lax.axis_index("x"), lax.axis_index("zq"), lax.axis_index(("zp", "yl"))
    tp = lax.axis_index(TP_AXES)
    info = jnp.stack([start_pos[0], x, zq, near]).astype(jnp.int32)

    own = []
    for g in range(KV_LOCAL):
        at = slice(g * 128, (g + 1) * 128)
        empty = jnp.zeros((TOK, 128), jnp.bfloat16)
        own.append(
            jnp.concatenate(
                [
                    jnp.concatenate([cache_keys[:, at], span_keys[:, at], empty], axis=0),
                    jnp.concatenate([cache_values[:, at], span_values[:, at], empty], axis=0),
                ],
                axis=1,
            )
        )
    following = [along(v, "zq", 1) for v in own]
    previous = [along(v, "zq", 3) for v in own]
    far = [along(following[0], "zq", 1), along(previous[1], "zq", 3)]
    parts = [v for g in range(KV_LOCAL) for v in (own[g], following[g], previous[g], far[g])]

    sizes = [lengths] + [along(lengths, "zq", k) for k in STEPS[1:]]
    packed = pack(queries, sizes)
    gathered = lax.all_to_all(packed, NEAR_AXES, 0, 0, tiled=True).reshape(GTOK, WIDTH + 128)

    wide = w_out.shape[0] // 2
    own_w = [w_out[:wide], w_out[wide:]]
    held = after(own_w[0], following[1], previous[1])
    next_a, last_a = along(held, "x", 1), along(held, "x", 3)
    held = after(own_w[1], next_a, last_a)
    next_b, last_b = along(held, "x", 1), along(held, "x", 3)
    far_a = along(after(next_a, next_b, last_b), "x", 1)
    far_b = along(after(last_b, next_b), "x", 3)
    weights = [(own_w[0], own_w[1]), (next_a, next_b), (far_a, far_b), (last_a, last_b)]

    partial = attend(info, gathered, parts)
    partial = after(partial, next_a, last_a)
    got = lax.all_to_all(
        partial.reshape(MEMBERS, TOK, WIDTH + 128), NEAR_AXES, 0, 0, tiled=True
    )
    copies = after(merge(got), next_b, last_b)
    merged = lax.all_to_all(copies, COLUMN_AXES, 0, 0, tiled=True).reshape(GTOK, WIDTH)

    projected = jnp.stack(
        [
            (
                jnp.dot(merged[:, :wide], a, preferred_element_type=jnp.float32)
                + jnp.dot(merged[:, wide:], b, preferred_element_type=jnp.float32)
            ).astype(jnp.bfloat16)
            for a, b in weights
        ]
    )
    total = None
    for r in range(X):
        block = lax.dynamic_index_in_dim(projected, (tp + r - x) % X, 0, keepdims=False)
        pairs = [(a * 4 + b, ((b + r) % X) * 4 + a) for a in range(X) for b in range(4)]
        term = lax.ppermute(block, ("x", "yh", "c"), pairs).astype(jnp.float32)
        total = term if total is None else total + term
    return total.astype(jnp.bfloat16)


def solution(mesh):
    fine = Mesh(mesh.devices.reshape(X, ZQ, ZP, YL, YH, CORE), CTX_AXES + TP_AXES)
    split = P(CTX_AXES, TP_AXES)
    return jax.shard_map(
        shards,
        mesh=fine,
        in_specs=(split, split, split, split, split, P(CTX_AXES), P(), P(TP_AXES, CTX_AXES)),
        out_specs=P(TP_AXES, CTX_AXES),
        check_vma=False,
    )
```

time: 236 us -> 186 us (0.79)
  blocking collectives: 57.3 us -> 0 us
  starting transfers between devices: 25.9 us -> 68.1 us
  waiting for transfers between devices: 110 us -> 85.1 us
  Pallas kernels: 27.9 us -> 19.4 us
    all_to_all x2 -> x0, blocking collectives: 57.3 us -> none  [the longest x1 35.1 us: shards(): lax.all_to_all(partial.reshape(ZY, TOK, WIDTH + 128), ZY_AXES, 0, 0, tile...]
    ppermute x6 -> x15, waiting for transfers between devices: 82.1 us -> 44.6 us  [along(): return lax.ppermute(v, axis, [((i + k) % 4, i) for i in range(4)])]
    all_to_all x2 -> x3, starting transfers between devices: 7.31 us -> 30.5 us  [the longest x1 15.4 us: shards(): lax.all_to_all(partial.reshape(MEMBERS, TOK, WIDTH + 128), NEAR_AXES, 0,...]
    ppermute x6 -> x15, starting transfers between devices: 8.46 us -> 29.4 us  [along(): return lax.ppermute(v, axis, [((i + k) % 4, i) for i in range(4)])]
    pallas_call x1, Pallas kernels: 26 us -> 14.4 us  [attend(): pl.pallas_call(attend_kernel, out_shape=jax.ShapeDtypeStruct((GTOK, WIDTH...]
    all_to_all x2 -> x3, waiting for transfers between devices: 24.4 us -> 34.6 us  [the longest x1 24.2 us: shards(): lax.all_to_all(copies, COLUMN_AXES, 0, 0, tiled=True).reshape(GTOK, WIDTH)]
    pallas_call x1 -> x2, Pallas kernels: 1.87 us -> 5 us  [the longest x1 3.12 us: pack(): pl.pallas_call(pack_kernel, out_shape=jax.ShapeDtypeStruct((MEMBERS, TOK,...]
    ppermute x4, waiting for transfers between devices: 3.2 us -> 5.9 us  [shards(): term = lax.ppermute(block, ('x', 'yh', 'c'), pairs).astype(jnp.float32)]
  transfers between devices with their start and end apart: 12 -> 22, of which waited for: 7 -> 11; matrix products, arithmetic and copies ran while one was open for 3% -> 5% of each run, Pallas kernels for 0% -> 9%
where the time goes in v2:
time: 186 us; the launch traced here: 185 us
  waiting for transfers between devices  85.1 us (46%)
  starting transfers between devices  68.1 us (37%)
  Pallas kernels  19.4 us (10%)
  matrix products  7.52 us (4%)
  local copies, waits for them, and re-layouts  2.46 us (1%)
    ppermute x15, waiting for transfers between devices, along(): return lax.ppermute(v, axis, [((i + k) % 4, i) for i in range(4)])  44.6 us
    ppermute x15, starting transfers between devices, along(): return lax.ppermute(v, axis, [((i + k) % 4, i) for i in range(4)])  29.4 us
    all_to_all x1, waiting for transfers between devices, shards(): lax.all_to_all(copies, COLUMN_AXES, 0, 0, tiled=True).reshape(GTOK, WIDTH)  24.2 us
    all_to_all x1, starting transfers between devices, shards(): lax.all_to_all(partial.reshape(MEMBERS, TOK, WIDTH + 128), NEAR_AXES, 0,...  15.4 us
    pallas_call x1, Pallas kernels, attend(): pl.pallas_call(attend_kernel, out_shape=jax.ShapeDtypeStruct((GTOK, WIDTH...  14.4 us
    all_to_all x1, waiting for transfers between devices, shards(): lax.all_to_all(partial.reshape(MEMBERS, TOK, WIDTH + 128), NEAR_AXES, 0,...  10.4 us
    all_to_all x1, starting transfers between devices, shards(): lax.all_to_all(copies, COLUMN_AXES, 0, 0, tiled=True).reshape(GTOK, WIDTH)  8.78 us
    ppermute x4, starting transfers between devices, shards(): term = lax.ppermute(block, ('x', 'yh', 'c'), pairs).astype(jnp.float32)  8.32 us
  transfers between devices with their start and end apart: 22, of which 11 were waited for; matrix products, arithmetic and copies ran while one was open for 5% of the time, Pallas kernels for 9%

profile of v2, /device:TPU:2, one launch (start us, length us, event | category | flops | bytes accessed | tf_op | source)
XLA Modules:
  0.0 185.2 jit_solution(2898139198582568602)
XLA Ops:
  0.0 3.3 %collective-permute-start.1 = (s32[1]{0:T(128)}, s32[1]{0:T(128)}, u32[]{:S(2)}, u32[]{:S(2)}) collective-permute-start(s32[1]{0:T(128)} %param.13), channel_id=1, source_target_pairs={{48,0},{0,16},{16,32},{32,48},{49,1},{1,17},{17,33},{33,49},{50,2}... | collective-permute-start | bytes 20 | tf_op jit(solution)/shard_map/ppermute | solution.py:209
  3.3 3.0 %collective-permute-start = (s32[1]{0:T(128)}, s32[1]{0:T(128)}, u32[]{:S(2)}, u32[]{:S(2)}) collective-permute-start(s32[1]{0:T(128)} %param.13), channel_id=1, source_target_pairs={{16,0},{32,16},{48,32},{0,48},{17,1},{33,17},{49,33},{1,49},{18,2}... | collective-permute-start | bytes 20 | tf_op jit(solution)/shard_map/ppermute | solution.py:209
  6.3 5.0 %collective-permute-start.2 = (s32[1]{0:T(128)}, s32[1]{0:T(128)}, u32[]{:S(2)}, u32[]{:S(2)}) collective-permute-start(s32[1]{0:T(128)} %param.13), channel_id=1, source_target_pairs={{32,0},{48,16},{0,32},{16,48},{33,1},{49,17},{1,33},{17,49},{34,2}... | collective-permute-start | bytes 20 | tf_op jit(solution)/shard_map/ppermute | solution.py:209
  12.0 1.8 collective-permute-done.2.size3
  14.7 3.1 %pack.1 = bf16[16,8,4224]{2,1,0:T(8,128)(2,1)} custom-call(bf16[8,4096]{1,0:T(8,128)(2,1)S(1)} %copy-done, s32[1]{0:T(128)S(6)} %copy.9.size0, s32[1]{0:T(128)} %collective-permute-done.size1, s32[1]{0:T(128)} %collective-permute-done.1.size2, s32[1]{0:T(128)} %collective-permute-done.2.size3), custom_call_target="tpu_custom_call" | custom-call | flops 524288 | bytes 1048576 | tf_op jit(solution)/shard_map/pack/pallas_call | solution.py:58
  17.8 6.3 %all-to-all-start = ((bf16[16,8,4224]{2,1,0:T(8,128)(2,1)}), bf16[16,8,4224]{2,1,0:T(8,128)(2,1)S(1)}, u32[]{:S(2)}, u32[]{:S(2)}) async-start(bf16[16,8,4224]{2,1,0:T(8,128)(2,1)} %pack.1), calls=%async_computation | async-start | bytes 2162688 | tf_op jit(solution)/shard_map/all_to_all | solution.py:241
  24.4 3.0 %collective-permute-start.3 = (bf16[528,256]{1,0:T(8,128)(2,1)S(1)}, bf16[528,256]{1,0:T(8,128)(2,1)S(1)}, u32[]{:S(2)}, u32[]{:S(2)}) collective-permute-start(bf16[528,256]{1,0:T(8,128)(2,1)S(1)} %get-tuple-element.31.refs_0_), channel_id=1, source_target_pairs={{16,0},{32,16},{48,32},{0,48},{17,1},{33,17},{49,33},{1,49},{18,2}... | collective-permute-start | bytes 811016 | tf_op jit(solution)/shard_map/ppermute | solution.py:209
  27.4 2.8 %collective-permute-start.4 = (bf16[528,256]{1,0:T(8,128)(2,1)S(1)}, bf16[528,256]{1,0:T(8,128)(2,1)S(1)}, u32[]{:S(2)}, u32[]{:S(2)}) collective-permute-start(bf16[528,256]{1,0:T(8,128)(2,1)S(1)} %get-tuple-element.31.refs_0_), channel_id=1, source_target_pairs={{48,0},{0,16},{16,32},{32,48},{49,1},{1,17},{17,33},{33,49},{50,2}... | collective-permute-start | bytes 811016 | tf_op jit(solution)/shard_map/ppermute | solution.py:209
  31.5 2.4 %collective-permute-done.3.refs_1_ = bf16[528,256]{1,0:T(8,128)(2,1)S(1)} collective-permute-done((bf16[528,256]{1,0:T(8,128)(2,1)S(1)}, bf16[528,256]{1,0:T(8,128)(2,1)S(1)}, u32[]{:S(2)}, u32[]{:S(2)}) %collective-permute-start.3) | collective-permute-done | bytes 270368 | tf_op jit(solution)/shard_map/ppermute | solution.py:209
  34.0 4.6 %collective-permute-start.5 = (bf16[528,256]{1,0:T(8,128)(2,1)S(1)}, bf16[528,256]{1,0:T(8,128)(2,1)S(1)}, u32[]{:S(2)}, u32[]{:S(2)}) collective-permute-start(bf16[528,256]{1,0:T(8,128)(2,1)S(1)} %collective-permute-done.3.refs_1_), channel_id=1, source_target_pairs={{16,0},{32,16},{48,32},{0,48},{17,1},{33,17},{49,33},{1,49},{18,2}... | collective-permute-start | bytes 811016 | tf_op jit(solution)/shard_map/ppermute | solution.py:209
  38.6 19.2 %collective-permute-done.7.refs_6_ = bf16[528,256]{1,0:T(8,128)(2,1)S(1)} collective-permute-done((bf16[528,256]{1,0:T(8,128)(2,1)S(1)}, bf16[528,256]{1,0:T(8,128)(2,1)S(1)}, u32[]{:S(2)}, u32[]{:S(2)}) %collective-permute-start.7) | collective-permute-done | bytes 270368 | tf_op jit(solution)/shard_map/ppermute | solution.py:209
  59.3 1.8 collective-permute-start.10
  63.5 3.0 %collective-permute-done.8.refs_7_ = bf16[528,256]{1,0:T(8,128)(2,1)S(1)} collective-permute-done((bf16[528,256]{1,0:T(8,128)(2,1)S(1)}, bf16[528,256]{1,0:T(8,128)(2,1)S(1)}, u32[]{:S(2)}, u32[]{:S(2)}) %collective-permute-start.8) | collective-permute-done | bytes 270368 | tf_op jit(solution)/shard_map/ppermute | solution.py:209
  66.5 14.4 %attend.1 = bf16[128,4224]{1,0:T(8,128)(2,1)} custom-call(s32[4]{0:T(128)S(1)} %pad_add_fusion.info, bf16[128,4224]{1,0:T(8,128)(2,1)S(1)} %bitcast.28, bf16[528,256]{1,0:T(8,128)(2,1)S(1)} %get-tuple-element.31.refs_0_, bf16[528,256]{1,0:T(8,128)(2,1)S(1)} %collective-permute-done.3.refs_1_, bf16[528,256]{1,0:T(8,128)(2,1)S(1)} %collective-permute-done.4.refs_2_, ...), custom_call_target="tpu_custom_call" | custom-call | flops 9126805504 | bytes 4194304 | tf_op jit(solution)/shard_map/attend/pallas_call | solution.py:164
  80.9 15.4 %all-to-all-start.1 = ((bf16[16,8,4224]{2,1,0:T(8,128)(2,1)}), bf16[16,8,4224]{2,1,0:T(8,128)(2,1)S(1)}, u32[]{:S(2)}, u32[]{:S(2)}) async-start(bf16[16,8,4224]{2,1,0:T(8,128)(2,1)} %bitcast.4), calls=%async_computation.1 | async-start | bytes 2162688 | tf_op jit(solution)/shard_map/all_to_all | solution.py:255
  98.4 10.4 %all-to-all-done.1.got = bf16[16,8,4224]{2,1,0:T(8,128)(2,1)S(1)} async-done(((bf16[16,8,4224]{2,1,0:T(8,128)(2,1)}), bf16[16,8,4224]{2,1,0:T(8,128)(2,1)S(1)}, u32[]{:S(2)}, u32[]{:S(2)}) %all-to-all-start.1) | async-done | bytes 1081376 | tf_op jit(solution)/shard_map/all_to_all | solution.py:255
  108.8 1.9 %merge.1 = bf16[16,8,4096]{2,1,0:T(8,128)(2,1)} custom-call(bf16[16,8,4224]{2,1,0:T(8,128)(2,1)S(1)} %all-to-all-done.1.got), custom_call_target="tpu_custom_call" | custom-call | flops 2097152 | bytes 2097152 | tf_op jit(solution)/shard_map/merge/pallas_call | solution.py:197
  110.7 15.5 %collective-permute-done.12 = bf16[2048,256]{1,0:T(8,128)(2,1)S(1)} collective-permute-done((bf16[2048,256]{1,0:T(8,128)(2,1)S(1)}, bf16[2048,256]{1,0:T(8,128)(2,1)S(1)}, u32[]{:S(2)}, u32[]{:S(2)}) %collective-permute-start.12) | collective-permute-done | bytes 1048608 | tf_op jit(solution)/shard_map/ppermute | solution.py:209
  127.4 8.8 %all-to-all-start.2 = ((bf16[16,8,4096]{2,1,0:T(8,128)(2,1)}), bf16[16,8,4096]{2,1,0:T(8,128)(2,1)S(1)}, u32[]{:S(2)}, u32[]{:S(2)}) async-start(bf16[16,8,4096]{2,1,0:T(8,128)(2,1)} %merge.1), calls=%async_computation.2 | async-start | bytes 2097152 | tf_op jit(solution)/shard_map/all_to_all | solution.py:259
  136.3 1.7 collective-permute-start.13
  138.4 24.2 %all-to-all-done.2 = bf16[16,8,4096]{2,1,0:T(8,128)(2,1)S(1)} async-done(((bf16[16,8,4096]{2,1,0:T(8,128)(2,1)}), bf16[16,8,4096]{2,1,0:T(8,128)(2,1)S(1)}, u32[]{:S(2)}, u32[]{:S(2)}) %all-to-all-start.2) | async-done | bytes 1048608 | tf_op jit(solution)/shard_map/all_to_all | solution.py:259
  170.2 1.9 %collective-permute-start.15 = (bf16[128,256]{1,0:T(8,128)(2,1)S(1)}, bf16[128,256]{1,0:T(8,128)(2,1)S(1)}, u32[]{:S(2)}, u32[]{:S(2)}) collective-permute-start(bf16[128,256]{1,0:T(8,128)(2,1)S(1)} %get-tuple-element.19), channel_id=1, source_target_pairs={{0,0},{1,64},{2,128},{3,192},{64,1},{65,65},{66,129},{67,193},{128... | collective-permute-start | bytes 196616 | tf_op jit(solution)/shard_map/ppermute | solution.py:274
  173.8 4.8 %collective-permute-start.17 = (bf16[128,256]{1,0:T(8,128)(2,1)S(1)}, bf16[128,256]{1,0:T(8,128)(2,1)S(1)}, u32[]{:S(2)}, u32[]{:S(2)}) collective-permute-start(bf16[128,256]{1,0:T(8,128)(2,1)S(1)} %get-tuple-element.21), channel_id=1, source_target_pairs={{0,128},{1,192},{2,0},{3,64},{64,129},{65,193},{66,1},{67,65},{128... | collective-permute-start | bytes 196616 | tf_op jit(solution)/shard_map/ppermute | solution.py:274
  180.2 4.3 %collective-permute-done.17 = bf16[128,256]{1,0:T(8,128)(2,1)S(1)} collective-permute-done((bf16[128,256]{1,0:T(8,128)(2,1)S(1)}, bf16[128,256]{1,0:T(8,128)(2,1)S(1)}, u32[]{:S(2)}, u32[]{:S(2)}) %collective-permute-start.17) | collective-permute-done | bytes 65568 | tf_op jit(solution)/shard_map/ppermute | solution.py:274
  (56 shorter events, 21.0 us)
Async XLA Ops:
  0.0 12.0 %collective-permute-start.1 = (s32[1]{0:T(128)}, s32[1]{0:T(128)}, u32[]{:S(2)}, u32[]{:S(2)}) collective-permute-start(s32[1]{0:T(128)} %param.13), channel_id=1, source_target_pairs={{48,0},{0,16},{16,32},{32,48},{49,1},{1,17},{17,33},{33,49},{50,2}... | collective-permute-start | bytes 20 | tf_op jit(solution)/shard_map/ppermute | solution.py:209
  3.3 8.8 %collective-permute-start = (s32[1]{0:T(128)}, s32[1]{0:T(128)}, u32[]{:S(2)}, u32[]{:S(2)}) collective-permute-start(s32[1]{0:T(128)} %param.13), channel_id=1, source_target_pairs={{16,0},{32,16},{48,32},{0,48},{17,1},{33,17},{49,33},{1,49},{18,2}... | collective-permute-start | bytes 20 | tf_op jit(solution)/shard_map/ppermute | solution.py:209
  6.3 7.5 %collective-permute-start.2 = (s32[1]{0:T(128)}, s32[1]{0:T(128)}, u32[]{:S(2)}, u32[]{:S(2)}) collective-permute-start(s32[1]{0:T(128)} %param.13), channel_id=1, source_target_pairs={{32,0},{48,16},{0,32},{16,48},{33,1},{49,17},{1,33},{17,49},{34,2}... | collective-permute-start | bytes 20 | tf_op jit(solution)/shard_map/ppermute | solution.py:209
  17.8 48.7 %all-to-all-start = ((bf16[16,8,4224]{2,1,0:T(8,128)(2,1)}), bf16[16,8,4224]{2,1,0:T(8,128)(2,1)S(1)}, u32[]{:S(2)}, u32[]{:S(2)}) async-start(bf16[16,8,4224]{2,1,0:T(8,128)(2,1)} %pack.1), calls=%async_computation | async-start | bytes 2162688 | tf_op jit(solution)/shard_map/all_to_all | solution.py:241
  24.1 33.7 %copy-start.1 = (bf16[4096,256]{1,0:T(8,128)(2,1)S(1)}, bf16[4096,256]{1,0:T(8,128)(2,1)}, u32[]{:S(2)}) copy-start(bf16[4096,256]{1,0:T(8,128)(2,1)} %param.15) | copy-start | bytes 6291460
  24.4 9.6 %collective-permute-start.3 = (bf16[528,256]{1,0:T(8,128)(2,1)S(1)}, bf16[528,256]{1,0:T(8,128)(2,1)S(1)}, u32[]{:S(2)}, u32[]{:S(2)}) collective-permute-start(bf16[528,256]{1,0:T(8,128)(2,1)S(1)} %get-tuple-element.31.refs_0_), channel_id=1, source_target_pairs={{16,0},{32,16},{48,32},{0,48},{17,1},{33,17},{49,33},{1,49},{18,2}... | collective-permute-start | bytes 811016 | tf_op jit(solution)/shard_map/ppermute | solution.py:209
  27.4 30.4 %collective-permute-start.7 = (bf16[528,256]{1,0:T(8,128)(2,1)S(1)}, bf16[528,256]{1,0:T(8,128)(2,1)S(1)}, u32[]{:S(2)}, u32[]{:S(2)}) collective-permute-start(bf16[528,256]{1,0:T(8,128)(2,1)S(1)} %get-tuple-element.32.refs_4_), channel_id=1, source_target_pairs={{48,0},{0,16},{16,32},{32,48},{49,1},{1,17},{17,33},{33,49},{50,2}... | collective-permute-start | bytes 811016 | tf_op jit(solution)/shard_map/ppermute | solution.py:209
  27.4 36.1 %collective-permute-start.4 = (bf16[528,256]{1,0:T(8,128)(2,1)S(1)}, bf16[528,256]{1,0:T(8,128)(2,1)S(1)}, u32[]{:S(2)}, u32[]{:S(2)}) collective-permute-start(bf16[528,256]{1,0:T(8,128)(2,1)S(1)} %get-tuple-element.31.refs_0_), channel_id=1, source_target_pairs={{48,0},{0,16},{16,32},{32,48},{49,1},{1,17},{17,33},{33,49},{50,2}... | collective-permute-start | bytes 811016 | tf_op jit(solution)/shard_map/ppermute | solution.py:209
  30.1 29.2 %collective-permute-start.6 = (bf16[528,256]{1,0:T(8,128)(2,1)S(1)}, bf16[528,256]{1,0:T(8,128)(2,1)S(1)}, u32[]{:S(2)}, u32[]{:S(2)}) collective-permute-start(bf16[528,256]{1,0:T(8,128)(2,1)S(1)} %get-tuple-element.32.refs_4_), channel_id=1, source_target_pairs={{16,0},{32,16},{48,32},{0,48},{17,1},{33,17},{49,33},{1,49},{18,2}... | collective-permute-start | bytes 811016 | tf_op jit(solution)/shard_map/ppermute | solution.py:209
  34.0 29.5 %collective-permute-start.5 = (bf16[528,256]{1,0:T(8,128)(2,1)S(1)}, bf16[528,256]{1,0:T(8,128)(2,1)S(1)}, u32[]{:S(2)}, u32[]{:S(2)}) collective-permute-start(bf16[528,256]{1,0:T(8,128)(2,1)S(1)} %collective-permute-done.3.refs_1_), channel_id=1, source_target_pairs={{16,0},{32,16},{48,32},{0,48},{17,1},{33,17},{49,33},{1,49},{18,2}... | collective-permute-start | bytes 811016 | tf_op jit(solution)/shard_map/ppermute | solution.py:209
  57.8 8.7 %collective-permute-start.8 = (bf16[528,256]{1,0:T(8,128)(2,1)S(1)}, bf16[528,256]{1,0:T(8,128)(2,1)S(1)}, u32[]{:S(2)}, u32[]{:S(2)}) collective-permute-start(bf16[528,256]{1,0:T(8,128)(2,1)S(1)} %collective-permute-done.7.refs_6_), channel_id=1, source_target_pairs={{48,0},{0,16},{16,32},{32,48},{49,1},{1,17},{17,33},{33,49},{50,2}... | collective-permute-start | bytes 811016 | tf_op jit(solution)/shard_map/ppermute | solution.py:209
  59.3 21.6 %collective-permute-start.10 = (bf16[2048,256]{1,0:T(8,128)(2,1)}, bf16[2048,256]{1,0:T(8,128)(2,1)}, u32[]{:S(2)}, u32[]{:S(2)}) collective-permute-start(bf16[2048,256]{1,0:T(8,128)(2,1)} %get-tuple-element.11), channel_id=1, source_target_pairs={{192,0},{0,64},{64,128},{128,192},{193,1},{1,65},{65,129},{129,193... | collective-permute-start | bytes 3145736 | tf_op jit(solution)/shard_map/ppermute | solution.py:209
  61.1 19.8 %collective-permute-start.9 = (bf16[2048,256]{1,0:T(8,128)(2,1)}, bf16[2048,256]{1,0:T(8,128)(2,1)}, u32[]{:S(2)}, u32[]{:S(2)}) collective-permute-start(bf16[2048,256]{1,0:T(8,128)(2,1)} %get-tuple-element.11), channel_id=1, source_target_pairs={{64,0},{128,64},{192,128},{0,192},{65,1},{129,65},{193,129},{1,193... | collective-permute-start | bytes 3145736 | tf_op jit(solution)/shard_map/ppermute | solution.py:209
  80.9 15.4 %copy-start.3 = (bf16[2048,256]{1,0:T(8,128)(2,1)S(1)}, bf16[2048,256]{1,0:T(8,128)(2,1)}, u32[]{:S(2)}) copy-start(bf16[2048,256]{1,0:T(8,128)(2,1)} %get-tuple-element.13) | copy-start | bytes 3145732
  80.9 27.9 %all-to-all-start.1 = ((bf16[16,8,4224]{2,1,0:T(8,128)(2,1)}), bf16[16,8,4224]{2,1,0:T(8,128)(2,1)S(1)}, u32[]{:S(2)}, u32[]{:S(2)}) async-start(bf16[16,8,4224]{2,1,0:T(8,128)(2,1)} %bitcast.4), calls=%async_computation.1 | async-start | bytes 2162688 | tf_op jit(solution)/shard_map/all_to_all | solution.py:255
  96.3 29.9 %collective-permute-start.12 = (bf16[2048,256]{1,0:T(8,128)(2,1)S(1)}, bf16[2048,256]{1,0:T(8,128)(2,1)S(1)}, u32[]{:S(2)}, u32[]{:S(2)}) collective-permute-start(bf16[2048,256]{1,0:T(8,128)(2,1)S(1)} %copy-done.3), channel_id=1, source_target_pairs={{192,0},{0,64},{64,128},{128,192},{193,1},{1,65},{65,129},{129,193... | collective-permute-start | bytes 3145736 | tf_op jit(solution)/shard_map/ppermute | solution.py:209
  97.8 29.6 %collective-permute-start.11 = (bf16[2048,256]{1,0:T(8,128)(2,1)S(1)}, bf16[2048,256]{1,0:T(8,128)(2,1)}, u32[]{:S(2)}, u32[]{:S(2)}) collective-permute-start(bf16[2048,256]{1,0:T(8,128)(2,1)S(1)} %copy-done.3), channel_id=1, source_target_pairs={{64,0},{128,64},{192,128},{0,192},{65,1},{129,65},{193,129},{1,193... | collective-permute-start | bytes 3145736 | tf_op jit(solution)/shard_map/ppermute | solution.py:209
  127.4 35.1 %all-to-all-start.2 = ((bf16[16,8,4096]{2,1,0:T(8,128)(2,1)}), bf16[16,8,4096]{2,1,0:T(8,128)(2,1)S(1)}, u32[]{:S(2)}, u32[]{:S(2)}) async-start(bf16[16,8,4096]{2,1,0:T(8,128)(2,1)} %merge.1), calls=%async_computation.2 | async-start | bytes 2097152 | tf_op jit(solution)/shard_map/all_to_all | solution.py:259
  136.3 33.6 %collective-permute-start.13 = (bf16[2048,256]{1,0:T(8,128)(2,1)}, bf16[2048,256]{1,0:T(8,128)(2,1)S(1)}, u32[]{:S(2)}, u32[]{:S(2)}) collective-permute-start(bf16[2048,256]{1,0:T(8,128)(2,1)} %collective-permute-done.9), channel_id=1, source_target_pairs={{64,0},{128,64},{192,128},{0,192},{65,1},{129,65},{193,129},{1,193... | collective-permute-start | bytes 3145736 | tf_op jit(solution)/shard_map/ppermute | solution.py:209
  138.0 30.3 %collective-permute-start.14 = (bf16[2048,256]{1,0:T(8,128)(2,1)S(1)}, bf16[2048,256]{1,0:T(8,128)(2,1)}, u32[]{:S(2)}, u32[]{:S(2)}) collective-permute-start(bf16[2048,256]{1,0:T(8,128)(2,1)S(1)} %collective-permute-done.12), channel_id=1, source_target_pairs={{192,0},{0,64},{64,128},{128,192},{193,1},{1,65},{65,129},{129,193... | collective-permute-start | bytes 3145736 | tf_op jit(solution)/shard_map/ppermute | solution.py:209
  170.2 8.3 %collective-permute-start.15 = (bf16[128,256]{1,0:T(8,128)(2,1)S(1)}, bf16[128,256]{1,0:T(8,128)(2,1)S(1)}, u32[]{:S(2)}, u32[]{:S(2)}) collective-permute-start(bf16[128,256]{1,0:T(8,128)(2,1)S(1)} %get-tuple-element.19), channel_id=1, source_target_pairs={{0,0},{1,64},{2,128},{3,192},{64,1},{65,65},{66,129},{67,193},{128... | collective-permute-start | bytes 196616 | tf_op jit(solution)/shard_map/ppermute | solution.py:274
  172.2 8.1 %collective-permute-start.18 = (bf16[128,256]{1,0:T(8,128)(2,1)S(1)}, bf16[128,256]{1,0:T(8,128)(2,1)S(1)}, u32[]{:S(2)}, u32[]{:S(2)}) collective-permute-start(bf16[128,256]{1,0:T(8,128)(2,1)S(1)} %get-tuple-element.20), channel_id=1, source_target_pairs={{0,192},{1,0},{2,64},{3,128},{64,193},{65,1},{66,65},{67,129},{128... | collective-permute-start | bytes 196616 | tf_op jit(solution)/shard_map/ppermute | solution.py:274
  173.8 10.7 %collective-permute-start.17 = (bf16[128,256]{1,0:T(8,128)(2,1)S(1)}, bf16[128,256]{1,0:T(8,128)(2,1)S(1)}, u32[]{:S(2)}, u32[]{:S(2)}) collective-permute-start(bf16[128,256]{1,0:T(8,128)(2,1)S(1)} %get-tuple-element.21), channel_id=1, source_target_pairs={{0,128},{1,192},{2,0},{3,64},{64,129},{65,193},{66,1},{67,65},{128... | collective-permute-start | bytes 196616 | tf_op jit(solution)/shard_map/ppermute | solution.py:274
  178.6 5.9 %collective-permute-start.16 = (bf16[128,256]{1,0:T(8,128)(2,1)S(1)}, bf16[128,256]{1,0:T(8,128)(2,1)S(1)}, u32[]{:S(2)}, u32[]{:S(2)}) collective-permute-start(bf16[128,256]{1,0:T(8,128)(2,1)S(1)} %get-tuple-element.22), channel_id=1, source_target_pairs={{0,64},{1,128},{2,192},{3,0},{64,65},{65,129},{66,193},{67,1},{128... | collective-permute-start | bytes 196616 | tf_op jit(solution)/shard_map/ppermute | solution.py:274
  (6 other events, 42.0 us)

commit v3 on v2

v3 whole, which is shorter than its diff:
```python
import math

import jax
import jax.numpy as jnp
from jax import lax
from jax.experimental import pallas as pl
from jax.experimental.pallas import tpu as pltpu
from jax.sharding import Mesh, PartitionSpec as P

HEADS = 128
KV_HEADS = 8
HEAD_DIM = 128
GROUP = HEADS // KV_HEADS
HIDE = -1e30
SCALE = 1.0 / math.sqrt(HEAD_DIM)
LOG2E = 1.4426950408889634

X, Z, YL, YH, CORE = 4, 8, 2, 2, 2
MEMBERS = Z * YL
CTX_AXES = ("x", "z", "yl")
TP_AXES = ("yh", "c")
ZY_AXES = ("z", "yl")
TOK = 8
ROWS = 512
SPAN = 16
GTOK = MEMBERS * TOK
KV_LOCAL = 2
HEADS_LOCAL = KV_LOCAL * GROUP
WIDTH = HEADS_LOCAL * HEAD_DIM
PARTS = X
CACHE = PARTS * ROWS
COLS = CACHE + 128
STEPS = (0, 1, 3, 2)


def step_of(k):
    return jnp.where(k == 2, 3, jnp.where(k == 3, 2, k))


def collect_kernel(cache_k, cache_v, span_k, span_v, own, sems):
    copies = []
    for side, cache in enumerate((cache_k, cache_v)):
        for g in range(KV_LOCAL):
            copies.append(
                pltpu.make_async_copy(
                    cache.at[:, pl.ds(g * 128, 128)],
                    own.at[pl.ds(g * (ROWS + SPAN), ROWS), pl.ds(side * 128, 128)],
                    sems.at[side * KV_LOCAL + g],
                )
            )
    for copy in copies:
        copy.start()
    empty = jnp.zeros((TOK, 256), jnp.float32)
    for side, span in enumerate((span_k, span_v)):
        padded = jnp.concatenate([span[...].astype(jnp.float32), empty], axis=0)
        padded = padded.astype(jnp.bfloat16)
        for g in range(KV_LOCAL):
            at = g * (ROWS + SPAN) + ROWS
            own[at : at + SPAN, side * 128 : side * 128 + 128] = padded[:, g * 128 : g * 128 + 128]
    for copy in copies:
        copy.wait()


def collect(cache_keys, cache_values, span_keys, span_values):
    vmem, either = pl.BlockSpec(memory_space=pltpu.VMEM), pl.BlockSpec(memory_space=pl.ANY)
    return pl.pallas_call(
        collect_kernel,
        out_shape=jax.ShapeDtypeStruct((KV_LOCAL * (ROWS + SPAN), 256), jnp.bfloat16),
        in_specs=[either, either, vmem, vmem],
        out_specs=vmem,
        scratch_shapes=[pltpu.SemaphoreType.DMA((2 * KV_LOCAL,))],
        compiler_params=pltpu.CompilerParams(vmem_limit_bytes=4 << 20),
        cost_estimate=pl.CostEstimate(flops=1 << 16, bytes_accessed=1 << 20, transcendentals=0),
        name="collect",
    )(cache_keys, cache_values, span_keys, span_values)


def pack_kernel(queries, size0, size1, size2, size3, later, message):
    del later
    lane = lax.broadcasted_iota(jnp.int32, (TOK, 128), 1)
    tail = jnp.zeros((TOK, 128), jnp.int32)
    for k, size in enumerate((size0, size1, size2, size3)):
        high = size[0] // 256
        tail = jnp.where(lane == k, high, tail)
        tail = jnp.where(lane == PARTS + k, size[0] - high * 256, tail)
    tail = tail.astype(jnp.float32).astype(jnp.bfloat16)
    message[:, :, 0:WIDTH] = jnp.broadcast_to(queries[...][None], (MEMBERS, TOK, WIDTH))
    message[:, :, WIDTH : WIDTH + 128] = jnp.broadcast_to(tail[None], (MEMBERS, TOK, 128))


def pack(queries, sizes, own):
    vmem = pl.BlockSpec(memory_space=pltpu.VMEM)
    smem = pl.BlockSpec(memory_space=pltpu.SMEM)
    return pl.pallas_call(
        pack_kernel,
        out_shape=jax.ShapeDtypeStruct((MEMBERS, TOK, WIDTH + 128), jnp.bfloat16),
        in_specs=[vmem] + [smem] * PARTS + [pl.BlockSpec(memory_space=pl.ANY)],
        out_specs=vmem,
        compiler_params=pltpu.CompilerParams(vmem_limit_bytes=4 << 20),
        cost_estimate=pl.CostEstimate(flops=1 << 19, bytes_accessed=1 << 20, transcendentals=0),
        name="pack",
    )(queries, *sizes, own)


def visible_rows(info, tail):
    lane = lax.broadcasted_iota(jnp.int32, (GTOK, 128), 1)
    row = lax.broadcasted_iota(jnp.int32, (GTOK, 128), 0)
    held = (row % TOK == 0) & (lane < 2 * PARTS)
    size = jnp.where(held, tail * jnp.where(lane < PARTS, 256.0, 1.0), 0.0)
    shard = ((info[1] + step_of(lane % PARTS)) % X) * MEMBERS + row // TOK
    start = info[0].astype(jnp.float32)
    out = []
    for k in range(PARTS):
        own = ((info[1] + STEPS[k]) % X) * MEMBERS + info[2]
        offset = jnp.sum(jnp.where(shard < own, size, 0.0), keepdims=True)
        filled = jnp.sum(jnp.where(shard == own, size, 0.0), keepdims=True)
        out.append(jnp.clip(start - offset, 0.0, filled))
    return out


def attend_kernel(info, q_ref, own, after_, before, far0, far1, *refs):
    out_ref, keys, values, seen = refs
    limits = visible_rows(info, q_ref[:, WIDTH : WIDTH + 128].astype(jnp.float32))
    both = ROWS + SPAN
    kvs = [ref.at[pl.ds(g * both, both)] for g in range(KV_LOCAL) for ref in (own, after_, before)]
    kvs = kvs[:3] + [far0] + kvs[3:] + [far1]
    lane = lax.broadcasted_iota(jnp.int32, (ROWS, 128), 1)
    row = lax.broadcasted_iota(jnp.int32, (ROWS, 128), 0).astype(jnp.float32)
    for k in range(PARTS):
        bias = jnp.where((lane == 0) & (row >= limits[k]), HIDE, 0.0).astype(jnp.bfloat16)
        for g in range(KV_LOCAL):
            kv = kvs[g * PARTS + k]
            at = pl.ds(k * ROWS, ROWS)
            keys[g, at, 0:128] = kv[0:ROWS, 0:128]
            keys[g, at, 128:256] = bias
            values[g, at, 0:128] = kv[0:ROWS, 128:256]
            at = pl.ds(CACHE + k * SPAN, SPAN)
            keys[g, at, 0:128] = kv[ROWS : ROWS + SPAN, 0:128]
            values[g, at, 0:128] = kv[ROWS : ROWS + SPAN, 128:256]
    lane = lax.broadcasted_iota(jnp.int32, (128, 128), 1)
    row = lax.broadcasted_iota(jnp.int32, (128, 128), 0)
    marks = jnp.where((row < 64) & (lane == 64 + row), 1.0, 0.0) + jnp.where(
        (row >= 64) & (lane == 0), HIDE, 0.0
    )
    for g in range(KV_LOCAL):
        keys[g, pl.ds(CACHE, 128), 128:256] = marks.astype(jnp.bfloat16)
        keys[g, pl.ds(CACHE + 64, 64), 0:128] = jnp.zeros((64, 128), jnp.bfloat16)
        values[g, pl.ds(CACHE + 64, 64), 0:128] = jnp.zeros((64, 128), jnp.bfloat16)
        values[g, :, 128:256] = jnp.ones((COLS, 128), jnp.bfloat16)
    slot = lane - 64
    part, inner = slot // SPAN, slot % SPAN
    shard = ((info[1] + step_of(part)) % X) * MEMBERS + info[2]
    hidden = (inner >= TOK) | (shard * TOK + inner > info[1] * GTOK + row)
    extra = jnp.where(lane == 0, 1.0, jnp.where((slot >= 0) & hidden, HIDE, 0.0))
    seen[...] = extra.astype(jnp.bfloat16)

    per = 2
    mask = jnp.concatenate([seen[...]] * per, axis=0)

    def one_group(g, stats):
        def columns(h):
            return pl.ds(pl.multiple_of((g * GROUP + h) * 128, 128), 128)

        def score(i):
            heads = [q_ref[:, columns(i * per + j)] for j in range(per)]
            query = jnp.concatenate([jnp.concatenate(heads, axis=0), mask], axis=1)
            return lax.dot_general(
                query, keys[g], (((1,), (1,)), ((), ())), preferred_element_type=jnp.float32
            )

        scores = score(0)
        for i in range(GROUP // per):
            later = score(i + 1) if i + 1 < GROUP // per else None
            top = jnp.max(scores, axis=1, keepdims=True)
            weights = jnp.exp2((scores - top) * (SCALE * LOG2E)).astype(jnp.bfloat16)
            both = jnp.dot(weights, values[g], preferred_element_type=jnp.float32)
            total = both[:, 128:256]
            outs = (both[:, 0:128] / total).astype(jnp.bfloat16)
            lse = top * SCALE + jnp.log(total)
            for j in range(per):
                h = i * per + j
                out_ref[:, columns(h)] = outs[j * GTOK : (j + 1) * GTOK]
                mine = lane % HEADS_LOCAL == g * GROUP + h
                stats = jnp.where(mine, lse[j * GTOK : (j + 1) * GTOK], stats)
            scores = later
        return stats

    stats = lax.fori_loop(0, KV_LOCAL, one_group, jnp.zeros((GTOK, 128), jnp.float32))
    high = stats.astype(jnp.bfloat16).astype(jnp.float32)
    rest = stats - high
    middle = rest.astype(jnp.bfloat16).astype(jnp.float32)
    low = rest - middle
    pieces = jnp.where(lane < HEADS_LOCAL, high, jnp.where(lane < 2 * HEADS_LOCAL, middle, low))
    out_ref[:, WIDTH : WIDTH + 128] = pieces.astype(jnp.bfloat16)


def attend(info, queries, parts):
    vmem = pl.BlockSpec(memory_space=pltpu.VMEM)
    return pl.pallas_call(
        attend_kernel,
        out_shape=jax.ShapeDtypeStruct((GTOK, WIDTH + 128), jnp.bfloat16),
        in_specs=[pl.BlockSpec(memory_space=pltpu.SMEM)] + [vmem] * 6,
        out_specs=vmem,
        scratch_shapes=[
            pltpu.VMEM((KV_LOCAL, COLS, 256), jnp.bfloat16),
            pltpu.VMEM((KV_LOCAL, COLS, 256), jnp.bfloat16),
            pltpu.VMEM((GTOK, 128), jnp.bfloat16),
        ],
        compiler_params=pltpu.CompilerParams(vmem_limit_bytes=20 << 20),
        cost_estimate=pl.CostEstimate(
            flops=8 * HEADS_LOCAL * GTOK * COLS * 128,
            bytes_accessed=4 << 20,
            transcendentals=HEADS_LOCAL * GTOK * COLS,
        ),
        name="attend",
    )(info, queries, *parts)


def merge_kernel(got, out_ref):
    pieces = got[:, :, WIDTH : WIDTH + 128].astype(jnp.float32)
    lse = pieces + (pltpu.roll(pieces, 96, 2) + pltpu.roll(pieces, 64, 2))
    share = jnp.exp(lse - jnp.max(lse, axis=0, keepdims=True))
    share = share / jnp.sum(share, axis=0, keepdims=True)
    for h in range(HEADS_LOCAL):
        at = slice(h * 128, (h + 1) * 128)
        merged = jnp.sum(share[:, :, h : h + 1] * got[:, :, at].astype(jnp.float32), axis=0)
        out_ref[:, :, at] = jnp.broadcast_to(merged.astype(jnp.bfloat16)[None], (MEMBERS, TOK, 128))


def merge(got):
    vmem = pl.BlockSpec(memory_space=pltpu.VMEM)
    return pl.pallas_call(
        merge_kernel,
        out_shape=jax.ShapeDtypeStruct((MEMBERS, TOK, WIDTH), jnp.bfloat16),
        in_specs=[vmem],
        out_specs=vmem,
        compiler_params=pltpu.CompilerParams(vmem_limit_bytes=6 << 20),
        cost_estimate=pl.CostEstimate(flops=2 << 20, bytes_accessed=2 << 20, transcendentals=4096),
        name="merge",
    )(got)


def project_kernel(info, merged, *refs):
    pieces, out_ref = iter(refs[:-1]), refs[-1]
    for k in range(X):
        total, at = None, 0
        while at < WIDTH:
            w = next(pieces)
            rows = w.shape[0]
            term = jnp.dot(merged[:, at : at + rows], w[...], preferred_element_type=jnp.float32)
            total = term if total is None else total + term
            at += rows
        out_ref[(k + info[0] - info[1] + X) % X] = total.astype(jnp.bfloat16)


def project(info, merged, weights):
    vmem = pl.BlockSpec(memory_space=pltpu.VMEM)
    pieces = [w for part in weights for w in part]
    return pl.pallas_call(
        project_kernel,
        out_shape=jax.ShapeDtypeStruct((X, GTOK, 256), jnp.bfloat16),
        in_specs=[pl.BlockSpec(memory_space=pltpu.SMEM)] + [vmem] * (1 + len(pieces)),
        out_specs=vmem,
        compiler_params=pltpu.CompilerParams(vmem_limit_bytes=12 << 20),
        cost_estimate=pl.CostEstimate(
            flops=2 * GTOK * WIDTH * 256 * X, bytes_accessed=10 << 20, transcendentals=0
        ),
        name="project",
    )(info, merged, *pieces)


def along(v, axis, k):
    return lax.ppermute(v, axis, [((i + k) % 4, i) for i in range(4)])


def after(v, *earlier):
    return lax.optimization_barrier((v, *earlier))[0]


def shards(queries, span_keys, span_values, cache_keys, cache_values, lengths, start_pos, w_out):
    x, zy = lax.axis_index("x"), lax.axis_index(ZY_AXES)
    tp = lax.axis_index(TP_AXES)
    info = jnp.stack([start_pos[0], x, zy]).astype(jnp.int32)

    sizes = [lengths] + [along(lengths, "x", k) for k in STEPS[1:]]
    own = collect(cache_keys, cache_values, span_keys, span_values)
    following, previous = along(own, "x", 1), along(own, "x", 3)
    far0 = along(following[: ROWS + SPAN], "x", 1)
    far1 = along(previous[ROWS + SPAN :], "x", 3)

    packed = pack(queries, sizes, own)
    gathered = lax.all_to_all(packed, ZY_AXES, 0, 0, tiled=True).reshape(GTOK, WIDTH + 128)

    half = WIDTH // 2
    own_w = [w_out[:half], w_out[half:]]
    held = after(own_w[0], far0, far1)
    next0, last0 = along(held, "x", 1), along(held, "x", 3)
    held = after(own_w[1], next0, last0)
    next1, last1 = along(held, "x", 1), along(held, "x", 3)
    far_w0 = along(after(next0, next1, last1), "x", 1)
    far_w1 = along(after(last1, next1), "x", 3)
    weights = [own_w, [next0, next1], [far_w0, far_w1], [last0, last1]]

    partial = attend(info, gathered, [own, following, previous, far0, far1])
    partial = after(partial, next0, last0)
    got = lax.all_to_all(partial.reshape(MEMBERS, TOK, WIDTH + 128), ZY_AXES, 0, 0, tiled=True)
    copies = after(merge(got), next1, last1)
    merged = lax.all_to_all(copies, ZY_AXES, 0, 0, tiled=True).reshape(GTOK, WIDTH)

    projected = project(jnp.stack([x, tp]).astype(jnp.int32), merged, weights)
    total = None
    for r in range(X):
        pairs = [(a * 4 + b, ((b + r) % X) * 4 + a) for a in range(X) for b in range(4)]
        term = lax.ppermute(projected[r], ("x", "yh", "c"), pairs).astype(jnp.float32)
        total = term if total is None else total + term
    return total.astype(jnp.bfloat16)


def solution(mesh):
    fine = Mesh(mesh.devices.reshape(X, Z, YL, YH, CORE), CTX_AXES + TP_AXES)
    split = P(CTX_AXES, TP_AXES)
    return jax.shard_map(
        shards,
        mesh=fine,
        in_specs=(split, split, split, split, split, P(CTX_AXES), P(), P(TP_AXES, CTX_AXES)),
        out_specs=P(TP_AXES, CTX_AXES),
        check_vma=False,
    )
```

time: 186 us -> 153 us (0.82)
  starting transfers between devices: 68.1 us -> 46.3 us
  waiting for transfers between devices: 85.1 us -> 69.3 us
  local copies, waits for them, and re-layouts: 2.46 us -> 11.1 us
  matrix products: 7.52 us -> 0 us
  Pallas kernels: 19.4 us -> 22.1 us
    ppermute x15 -> x13, starting transfers between devices: 29.4 us -> 15.7 us  [along(): return lax.ppermute(v, axis, [((i + k) % 4, i) for i in range(4)])]
    all_to_all x3, starting transfers between devices: 30.5 us -> 20.7 us  [the longest x1 9.44 us: shards(): lax.all_to_all(packed, ZY_AXES, 0, 0, tiled=True).reshape(GTOK, WIDTH + 128)]
    unnamed x16 -> x22, local copies, waits for them, and re-layouts: 0.87 us -> 9.41 us
    all_to_all x3, waiting for transfers between devices: 34.6 us -> 26.5 us  [the longest x1 22.1 us: shards(): lax.all_to_all(partial.reshape(MEMBERS, TOK, WIDTH + 128), ZY_AXES, 0, 0,...]
    dot_general x8 -> x0, matrix products: 7.52 us -> none  [the longest x4 3.84 us: shards(): jnp.dot(merged[:, :wide], a, preferred_element_type=jnp.float32)]
    ppermute x15 -> x13, waiting for transfers between devices: 44.6 us -> 38.4 us  [along(): return lax.ppermute(v, axis, [((i + k) % 4, i) for i in range(4)])]
    pallas_call x0 -> x2, Pallas kernels: none -> 4.2 us  [the longest x1 4.06 us: project(): pl.pallas_call(project_kernel, out_shape=jax.ShapeDtypeStruct((X, GTOK, 2...]
  transfers between devices with their start and end apart: 22 -> 20, of which waited for: 11 -> 10; matrix products, arithmetic and copies ran while one was open for 5% -> 1% of each run, Pallas kernels for 9% -> 10%
where the time goes in v3:
time: 153 us; the launch traced here: 151 us
  waiting for transfers between devices  69.3 us (45%)
  starting transfers between devices  46.3 us (30%)
  Pallas kernels  22.1 us (14%)
  local copies, waits for them, and re-layouts  11.1 us (7%)
    ppermute x13, waiting for transfers between devices, along(): return lax.ppermute(v, axis, [((i + k) % 4, i) for i in range(4)])  38.4 us
    all_to_all x1, waiting for transfers between devices, shards(): lax.all_to_all(partial.reshape(MEMBERS, TOK, WIDTH + 128), ZY_AXES, 0, 0,...  22.1 us
    ppermute x13, starting transfers between devices, along(): return lax.ppermute(v, axis, [((i + k) % 4, i) for i in range(4)])  15.7 us
    pallas_call x1, Pallas kernels, attend(): pl.pallas_call(attend_kernel, out_shape=jax.ShapeDtypeStruct((GTOK, WIDTH...  14.1 us
    ppermute x4, starting transfers between devices, shards(): lax.ppermute(projected[r], ('x', 'yh', 'c'), pairs).astype(jnp.float32)  9.86 us
    all_to_all x1, starting transfers between devices, shards(): lax.all_to_all(packed, ZY_AXES, 0, 0, tiled=True).reshape(GTOK, WIDTH + 128)  9.44 us
    unnamed x22, local copies, waits for them, and re-layouts  9.41 us
    all_to_all x1, starting transfers between devices, shards(): lax.all_to_all(partial.reshape(MEMBERS, TOK, WIDTH + 128), ZY_AXES, 0, 0,...  7.44 us
  transfers between devices with their start and end apart: 20, of which 10 were waited for; matrix products, arithmetic and copies ran while one was open for 1% of the time, Pallas kernels for 10%

profile of v3, /device:TPU:2, one launch (start us, length us, event | category | flops | bytes accessed | tf_op | source)
XLA Modules:
  0.0 151.2 jit_solution(1357711340801418006)
XLA Ops:
  0.0 1.5 collective-permute-start.1
  2.3 2.1 %collective-permute-start.2 = (s32[1]{0:T(128)}, s32[1]{0:T(128)}, u32[]{:S(2)}, u32[]{:S(2)}) collective-permute-start(s32[1]{0:T(128)} %param.13), channel_id=1, source_target_pairs={{128,0},{192,64},{0,128},{64,192},{129,1},{193,65},{1,129},{65,193... | collective-permute-start | bytes 20 | tf_op jit(solution)/shard_map/ppermute | solution.py:273
  9.1 3.0 %pack.1 = bf16[16,8,4224]{2,1,0:T(8,128)(2,1)} custom-call(bf16[8,4096]{1,0:T(8,128)(2,1)S(1)} %copy-done.6, s32[1]{0:T(128)S(6)} %copy.9.size0, s32[1]{0:T(128)} %collective-permute-done.size1, s32[1]{0:T(128)} %collective-permute-done.1.size2, s32[1]{0:T(128)} %collective-permute-done.2.size3, bf16[1056,256]{1,0:T(8,128)(2,1)S(1)} %collect.1.later.own), custom_call_target="tpu_custom_call" | custom-call | flops 524288 | bytes 1048576 | tf_op jit(solution)/shard_map/pack/pallas_call | solution.py:94
  12.1 9.4 %all-to-all-start = ((bf16[16,8,4224]{2,1,0:T(8,128)(2,1)}), bf16[16,8,4224]{2,1,0:T(8,128)(2,1)}, u32[]{:S(2)}, u32[]{:S(2)}) async-start(bf16[16,8,4224]{2,1,0:T(8,128)(2,1)} %pack.1), calls=%async_computation | async-start | bytes 2162688 | tf_op jit(solution)/shard_map/all_to_all | solution.py:292
  23.7 10.9 %collective-permute-done.4.before = bf16[1056,256]{1,0:T(8,128)(2,1)S(1)} collective-permute-done((bf16[1056,256]{1,0:T(8,128)(2,1)S(1)}, bf16[1056,256]{1,0:T(8,128)(2,1)S(1)}, u32[]{:S(2)}, u32[]{:S(2)}) %collective-permute-start.4) | collective-permute-done | bytes 540704 | tf_op jit(solution)/shard_map/ppermute | solution.py:273
  36.6 1.6 %collective-permute-start.5 = (bf16[528,256]{1,0:T(8,128)(2,1)S(1)}, bf16[528,256]{1,0:T(8,128)(2,1)S(1)}, u32[]{:S(2)}, u32[]{:S(2)}) collective-permute-start(bf16[528,256]{1,0:T(8,128)(2,1)S(1)} %slice.32), channel_id=1, source_target_pairs={{64,0},{128,64},{192,128},{0,192},{65,1},{129,65},{193,129},{1,193... | collective-permute-start | bytes 811016 | tf_op jit(solution)/shard_map/ppermute | solution.py:273
  38.1 1.7 %fusion = (bf16[2048,256]{1,0:T(8,128)(2,1)S(1)}, bf16[2048,256]{1,0:T(8,128)(2,1)S(1)}) fusion(bf16[4096,256]{1,0:T(8,128)(2,1)} %param.15), kind=kLoop, calls=%fused_computation.7 | loop fusion | bytes 4194304 | tf_op jit(solution)/shard_map/slice | solution.py:295
  39.8 2.0 %collective-permute-done.6.far1 = bf16[528,256]{1,0:T(8,128)(2,1)S(1)} collective-permute-done((bf16[528,256]{1,0:T(8,128)(2,1)S(1)}, bf16[528,256]{1,0:T(8,128)(2,1)S(1)}, u32[]{:S(2)}, u32[]{:S(2)}) %collective-permute-start.6) | collective-permute-done | bytes 270368 | tf_op jit(solution)/shard_map/ppermute | solution.py:273
  43.7 2.2 %collective-permute-start.8 = (bf16[2048,256]{1,0:T(8,128)(2,1)S(1)}, bf16[2048,256]{1,0:T(8,128)(2,1)}, u32[]{:S(2)}, u32[]{:S(2)}) collective-permute-start(bf16[2048,256]{1,0:T(8,128)(2,1)S(1)} %get-tuple-element.11.refs_0_), channel_id=1, source_target_pairs={{192,0},{0,64},{64,128},{128,192},{193,1},{1,65},{65,129},{129,193... | collective-permute-start | bytes 3145736 | tf_op jit(solution)/shard_map/ppermute | solution.py:273
  46.8 3.0 %all-to-all-done = bf16[16,8,4224]{2,1,0:T(8,128)(2,1)} async-done(((bf16[16,8,4224]{2,1,0:T(8,128)(2,1)}), bf16[16,8,4224]{2,1,0:T(8,128)(2,1)}, u32[]{:S(2)}, u32[]{:S(2)}) %all-to-all-start) | async-done | bytes 1081376 | tf_op jit(solution)/shard_map/all_to_all | solution.py:292
  51.8 14.1 %attend.1 = bf16[128,4224]{1,0:T(8,128)(2,1)S(1)} custom-call(s32[3]{0:T(128)S(1)} %pad_add_fusion.1.info, bf16[128,4224]{1,0:T(8,128)(2,1)} %bitcast.3.q_ref, bf16[1056,256]{1,0:T(8,128)(2,1)S(1)} %collect.1.later.own, bf16[1056,256]{1,0:T(8,128)(2,1)S(1)} %copy-done.5, bf16[1056,256]{1,0:T(8,128)(2,1)S(1)} %collective-permute-done.4.before, ...), custom_call_target="tpu_custom_call" | custom-call | flops 9126805504 | bytes 4194304 | tf_op jit(solution)/shard_map/attend/pallas_call | solution.py:199
  67.0 2.2 %collective-permute-done.7.refs_2_ = bf16[2048,256]{1,0:T(8,128)(2,1)} collective-permute-done((bf16[2048,256]{1,0:T(8,128)(2,1)S(1)}, bf16[2048,256]{1,0:T(8,128)(2,1)}, u32[]{:S(2)}, u32[]{:S(2)}) %collective-permute-start.7) | collective-permute-done | bytes 1048608 | tf_op jit(solution)/shard_map/ppermute | solution.py:273
  69.2 7.4 %all-to-all-start.1 = ((bf16[16,8,4224]{2,1,0:T(8,128)(2,1)}), bf16[16,8,4224]{2,1,0:T(8,128)(2,1)S(1)}, u32[]{:S(2)}, u32[]{:S(2)}) async-start(bf16[16,8,4224]{2,1,0:T(8,128)(2,1)} %bitcast.15), calls=%async_computation.1 | async-start | bytes 2162688 | tf_op jit(solution)/shard_map/all_to_all | solution.py:306
  76.6 1.8 %collective-permute-start.10 = (bf16[2048,256]{1,0:T(8,128)(2,1)S(1)}, bf16[2048,256]{1,0:T(8,128)(2,1)}, u32[]{:S(2)}, u32[]{:S(2)}) collective-permute-start(bf16[2048,256]{1,0:T(8,128)(2,1)S(1)} %get-tuple-element.13.refs_1_), channel_id=1, source_target_pairs={{192,0},{0,64},{64,128},{128,192},{193,1},{1,65},{65,129},{129,193... | collective-permute-start | bytes 3145736 | tf_op jit(solution)/shard_map/ppermute | solution.py:273
  78.7 22.1 %all-to-all-done.1.got = bf16[16,8,4224]{2,1,0:T(8,128)(2,1)S(1)} async-done(((bf16[16,8,4224]{2,1,0:T(8,128)(2,1)}), bf16[16,8,4224]{2,1,0:T(8,128)(2,1)S(1)}, u32[]{:S(2)}, u32[]{:S(2)}) %all-to-all-start.1) | async-done | bytes 1081376 | tf_op jit(solution)/shard_map/all_to_all | solution.py:306
  102.6 3.9 %all-to-all-start.2 = ((bf16[16,8,4096]{2,1,0:T(8,128)(2,1)}), bf16[16,8,4096]{2,1,0:T(8,128)(2,1)S(1)}, u32[]{:S(2)}, u32[]{:S(2)}) async-start(bf16[16,8,4096]{2,1,0:T(8,128)(2,1)} %copy-done), calls=%async_computation.2 | async-start | bytes 2097152 | tf_op jit(solution)/shard_map/all_to_all | solution.py:308
  108.7 20.3 %collective-permute-done.11.refs_4_ = bf16[2048,256]{1,0:T(8,128)(2,1)} collective-permute-done((bf16[2048,256]{1,0:T(8,128)(2,1)}, bf16[2048,256]{1,0:T(8,128)(2,1)}, u32[]{:S(2)}, u32[]{:S(2)}) %collective-permute-start.11) | collective-permute-done | bytes 1048608 | tf_op jit(solution)/shard_map/ppermute | solution.py:273
  129.0 1.8 %collective-permute-done.12.refs_5_ = bf16[2048,256]{1,0:T(8,128)(2,1)} collective-permute-done((bf16[2048,256]{1,0:T(8,128)(2,1)}, bf16[2048,256]{1,0:T(8,128)(2,1)}, u32[]{:S(2)}, u32[]{:S(2)}) %collective-permute-start.12) | collective-permute-done | bytes 1048608 | tf_op jit(solution)/shard_map/ppermute | solution.py:273
  130.8 1.3 all-to-all-done.2
  132.2 4.1 %project.1 = bf16[4,128,256]{2,1,0:T(8,128)(2,1)S(1)} custom-call(s32[2]{0:T(128)S(1)} %pad_add_fusion.info, bf16[128,4096]{1,0:T(8,128)(2,1)S(1)} %bitcast.14, bf16[2048,256]{1,0:T(8,128)(2,1)S(1)} %get-tuple-element.11.refs_0_, bf16[2048,256]{1,0:T(8,128)(2,1)S(1)} %get-tuple-element.13.refs_1_, bf16[2048,256]{1,0:T(8,128)(2,1)} %collective-permute-done.7.refs_2_, ...), custom_call_target="tpu_custom_call" | custom-call | flops 1073741824 | bytes 10485760 | tf_op jit(solution)/shard_map/project/pallas_call | solution.py:259
  136.3 1.9 %collective-permute-start.13 = (bf16[128,256]{1,0:T(8,128)(2,1)S(1)}, bf16[128,256]{1,0:T(8,128)(2,1)S(1)}, u32[]{:S(2)}, u32[]{:S(2)}) collective-permute-start(bf16[128,256]{1,0:T(8,128)(2,1)S(1)} %get-tuple-element.19), channel_id=1, source_target_pairs={{0,0},{1,64},{2,128},{3,192},{64,1},{65,65},{66,129},{67,193},{128... | collective-permute-start | bytes 196616 | tf_op jit(solution)/shard_map/ppermute | solution.py:314
  139.0 4.4 %collective-permute-start.15 = (bf16[128,256]{1,0:T(8,128)(2,1)S(1)}, bf16[128,256]{1,0:T(8,128)(2,1)S(1)}, u32[]{:S(2)}, u32[]{:S(2)}) collective-permute-start(bf16[128,256]{1,0:T(8,128)(2,1)S(1)} %get-tuple-element.21), channel_id=1, source_target_pairs={{0,128},{1,192},{2,0},{3,64},{64,129},{65,193},{66,1},{67,65},{128... | collective-permute-start | bytes 196616 | tf_op jit(solution)/shard_map/ppermute | solution.py:314
  143.4 2.7 %collective-permute-start.14 = (bf16[128,256]{1,0:T(8,128)(2,1)S(1)}, bf16[128,256]{1,0:T(8,128)(2,1)S(1)}, u32[]{:S(2)}, u32[]{:S(2)}) collective-permute-start(bf16[128,256]{1,0:T(8,128)(2,1)S(1)} %get-tuple-element.22), channel_id=1, source_target_pairs={{0,64},{1,128},{2,192},{3,0},{64,65},{65,129},{66,193},{67,1},{128... | collective-permute-start | bytes 196616 | tf_op jit(solution)/shard_map/ppermute | solution.py:314
  146.1 4.4 %collective-permute-done.15 = bf16[128,256]{1,0:T(8,128)(2,1)S(1)} collective-permute-done((bf16[128,256]{1,0:T(8,128)(2,1)S(1)}, bf16[128,256]{1,0:T(8,128)(2,1)S(1)}, u32[]{:S(2)}, u32[]{:S(2)}) %collective-permute-start.15) | collective-permute-done | bytes 65568 | tf_op jit(solution)/shard_map/ppermute | solution.py:314
  (50 shorter events, 19.8 us)
Async XLA Ops:
  0.0 8.5 %collective-permute-start.1 = (s32[1]{0:T(128)}, s32[1]{0:T(128)}, u32[]{:S(2)}, u32[]{:S(2)}) collective-permute-start(s32[1]{0:T(128)} %param.13), channel_id=1, source_target_pairs={{192,0},{0,64},{64,128},{128,192},{193,1},{1,65},{65,129},{129,193... | collective-permute-start | bytes 20 | tf_op jit(solution)/shard_map/ppermute | solution.py:273
  1.5 7.0 %collective-permute-start = (s32[1]{0:T(128)}, s32[1]{0:T(128)}, u32[]{:S(2)}, u32[]{:S(2)}) collective-permute-start(s32[1]{0:T(128)} %param.13), channel_id=1, source_target_pairs={{64,0},{128,64},{192,128},{0,192},{65,1},{129,65},{193,129},{1,193... | collective-permute-start | bytes 20 | tf_op jit(solution)/shard_map/ppermute | solution.py:273
  2.3 6.2 %collective-permute-start.2 = (s32[1]{0:T(128)}, s32[1]{0:T(128)}, u32[]{:S(2)}, u32[]{:S(2)}) collective-permute-start(s32[1]{0:T(128)} %param.13), channel_id=1, source_target_pairs={{128,0},{192,64},{0,128},{64,192},{129,1},{193,65},{1,129},{65,193... | collective-permute-start | bytes 20 | tf_op jit(solution)/shard_map/ppermute | solution.py:273
  12.1 37.7 %all-to-all-start = ((bf16[16,8,4224]{2,1,0:T(8,128)(2,1)}), bf16[16,8,4224]{2,1,0:T(8,128)(2,1)}, u32[]{:S(2)}, u32[]{:S(2)}) async-start(bf16[16,8,4224]{2,1,0:T(8,128)(2,1)} %pack.1), calls=%async_computation | async-start | bytes 2162688 | tf_op jit(solution)/shard_map/all_to_all | solution.py:292
  21.6 13.0 %collective-permute-start.4 = (bf16[1056,256]{1,0:T(8,128)(2,1)S(1)}, bf16[1056,256]{1,0:T(8,128)(2,1)S(1)}, u32[]{:S(2)}, u32[]{:S(2)}) collective-permute-start(bf16[1056,256]{1,0:T(8,128)(2,1)S(1)} %collect.1.later.own), channel_id=1, source_target_pairs={{192,0},{0,64},{64,128},{128,192},{193,1},{1,65},{65,129},{129,193... | collective-permute-start | bytes 1622024 | tf_op jit(solution)/shard_map/ppermute | solution.py:273
  22.8 13.0 %collective-permute-start.3 = (bf16[1056,256]{1,0:T(8,128)(2,1)S(1)}, bf16[1056,256]{1,0:T(8,128)(2,1)S(1)}, u32[]{:S(2)}, u32[]{:S(2)}) collective-permute-start(bf16[1056,256]{1,0:T(8,128)(2,1)S(1)} %collect.1.later.own), channel_id=1, source_target_pairs={{64,0},{128,64},{192,128},{0,192},{65,1},{129,65},{193,129},{1,193... | collective-permute-start | bytes 1622024 | tf_op jit(solution)/shard_map/ppermute | solution.py:273
  34.6 7.3 %collective-permute-start.6 = (bf16[528,256]{1,0:T(8,128)(2,1)S(1)}, bf16[528,256]{1,0:T(8,128)(2,1)S(1)}, u32[]{:S(2)}, u32[]{:S(2)}) collective-permute-start(bf16[528,256]{1,0:T(8,128)(2,1)S(1)} %slice.33), channel_id=1, source_target_pairs={{192,0},{0,64},{64,128},{128,192},{193,1},{1,65},{65,129},{129,193... | collective-permute-start | bytes 811016 | tf_op jit(solution)/shard_map/ppermute | solution.py:273
  36.6 6.5 %collective-permute-start.5 = (bf16[528,256]{1,0:T(8,128)(2,1)S(1)}, bf16[528,256]{1,0:T(8,128)(2,1)S(1)}, u32[]{:S(2)}, u32[]{:S(2)}) collective-permute-start(bf16[528,256]{1,0:T(8,128)(2,1)S(1)} %slice.32), channel_id=1, source_target_pairs={{64,0},{128,64},{192,128},{0,192},{65,1},{129,65},{193,129},{1,193... | collective-permute-start | bytes 811016 | tf_op jit(solution)/shard_map/ppermute | solution.py:273
  43.7 23.2 %collective-permute-start.8 = (bf16[2048,256]{1,0:T(8,128)(2,1)S(1)}, bf16[2048,256]{1,0:T(8,128)(2,1)}, u32[]{:S(2)}, u32[]{:S(2)}) collective-permute-start(bf16[2048,256]{1,0:T(8,128)(2,1)S(1)} %get-tuple-element.11.refs_0_), channel_id=1, source_target_pairs={{192,0},{0,64},{64,128},{128,192},{193,1},{1,65},{65,129},{129,193... | collective-permute-start | bytes 3145736 | tf_op jit(solution)/shard_map/ppermute | solution.py:273
  45.9 23.2 %collective-permute-start.7 = (bf16[2048,256]{1,0:T(8,128)(2,1)S(1)}, bf16[2048,256]{1,0:T(8,128)(2,1)}, u32[]{:S(2)}, u32[]{:S(2)}) collective-permute-start(bf16[2048,256]{1,0:T(8,128)(2,1)S(1)} %get-tuple-element.11.refs_0_), channel_id=1, source_target_pairs={{64,0},{128,64},{192,128},{0,192},{65,1},{129,65},{193,129},{1,193... | collective-permute-start | bytes 3145736 | tf_op jit(solution)/shard_map/ppermute | solution.py:273
  49.8 1.0 copy-start.5
  50.9 1.0 copy-start.10
  65.9 1.0 copy-start.1
  69.2 31.6 %all-to-all-start.1 = ((bf16[16,8,4224]{2,1,0:T(8,128)(2,1)}), bf16[16,8,4224]{2,1,0:T(8,128)(2,1)S(1)}, u32[]{:S(2)}, u32[]{:S(2)}) async-start(bf16[16,8,4224]{2,1,0:T(8,128)(2,1)} %bitcast.15), calls=%async_computation.1 | async-start | bytes 2162688 | tf_op jit(solution)/shard_map/all_to_all | solution.py:306
  76.6 26.0 %collective-permute-start.10 = (bf16[2048,256]{1,0:T(8,128)(2,1)S(1)}, bf16[2048,256]{1,0:T(8,128)(2,1)}, u32[]{:S(2)}, u32[]{:S(2)}) collective-permute-start(bf16[2048,256]{1,0:T(8,128)(2,1)S(1)} %get-tuple-element.13.refs_1_), channel_id=1, source_target_pairs={{192,0},{0,64},{64,128},{128,192},{193,1},{1,65},{65,129},{129,193... | collective-permute-start | bytes 3145736 | tf_op jit(solution)/shard_map/ppermute | solution.py:273
  78.4 24.2 %collective-permute-start.9 = (bf16[2048,256]{1,0:T(8,128)(2,1)S(1)}, bf16[2048,256]{1,0:T(8,128)(2,1)}, u32[]{:S(2)}, u32[]{:S(2)}) collective-permute-start(bf16[2048,256]{1,0:T(8,128)(2,1)S(1)} %get-tuple-element.13.refs_1_), channel_id=1, source_target_pairs={{64,0},{128,64},{192,128},{0,192},{65,1},{129,65},{193,129},{1,193... | collective-permute-start | bytes 3145736 | tf_op jit(solution)/shard_map/ppermute | solution.py:273
  101.7 1.0 copy-start
  102.6 29.5 %all-to-all-start.2 = ((bf16[16,8,4096]{2,1,0:T(8,128)(2,1)}), bf16[16,8,4096]{2,1,0:T(8,128)(2,1)S(1)}, u32[]{:S(2)}, u32[]{:S(2)}) async-start(bf16[16,8,4096]{2,1,0:T(8,128)(2,1)} %copy-done), calls=%async_computation.2 | async-start | bytes 2097152 | tf_op jit(solution)/shard_map/all_to_all | solution.py:308
  106.5 22.5 %collective-permute-start.11 = (bf16[2048,256]{1,0:T(8,128)(2,1)}, bf16[2048,256]{1,0:T(8,128)(2,1)}, u32[]{:S(2)}, u32[]{:S(2)}) collective-permute-start(bf16[2048,256]{1,0:T(8,128)(2,1)} %collective-permute-done.7.refs_2_), channel_id=1, source_target_pairs={{64,0},{128,64},{192,128},{0,192},{65,1},{129,65},{193,129},{1,193... | collective-permute-start | bytes 3145736 | tf_op jit(solution)/shard_map/ppermute | solution.py:273
  107.8 23.0 %collective-permute-start.12 = (bf16[2048,256]{1,0:T(8,128)(2,1)}, bf16[2048,256]{1,0:T(8,128)(2,1)}, u32[]{:S(2)}, u32[]{:S(2)}) collective-permute-start(bf16[2048,256]{1,0:T(8,128)(2,1)} %collective-permute-done.10.refs_7_), channel_id=1, source_target_pairs={{192,0},{0,64},{64,128},{128,192},{193,1},{1,65},{65,129},{129,193... | collective-permute-start | bytes 3145736 | tf_op jit(solution)/shard_map/ppermute | solution.py:273
  136.3 9.9 %collective-permute-start.13 = (bf16[128,256]{1,0:T(8,128)(2,1)S(1)}, bf16[128,256]{1,0:T(8,128)(2,1)S(1)}, u32[]{:S(2)}, u32[]{:S(2)}) collective-permute-start(bf16[128,256]{1,0:T(8,128)(2,1)S(1)} %get-tuple-element.19), channel_id=1, source_target_pairs={{0,0},{1,64},{2,128},{3,192},{64,1},{65,65},{66,129},{67,193},{128... | collective-permute-start | bytes 196616 | tf_op jit(solution)/shard_map/ppermute | solution.py:314
  138.2 8.0 %collective-permute-start.16 = (bf16[128,256]{1,0:T(8,128)(2,1)S(1)}, bf16[128,256]{1,0:T(8,128)(2,1)S(1)}, u32[]{:S(2)}, u32[]{:S(2)}) collective-permute-start(bf16[128,256]{1,0:T(8,128)(2,1)S(1)} %get-tuple-element.20), channel_id=1, source_target_pairs={{0,192},{1,0},{2,64},{3,128},{64,193},{65,1},{66,65},{67,129},{128... | collective-permute-start | bytes 196616 | tf_op jit(solution)/shard_map/ppermute | solution.py:314
  139.0 11.5 %collective-permute-start.15 = (bf16[128,256]{1,0:T(8,128)(2,1)S(1)}, bf16[128,256]{1,0:T(8,128)(2,1)S(1)}, u32[]{:S(2)}, u32[]{:S(2)}) collective-permute-start(bf16[128,256]{1,0:T(8,128)(2,1)S(1)} %get-tuple-element.21), channel_id=1, source_target_pairs={{0,128},{1,192},{2,0},{3,64},{64,129},{65,193},{66,1},{67,65},{128... | collective-permute-start | bytes 196616 | tf_op jit(solution)/shard_map/ppermute | solution.py:314
  143.4 7.1 %collective-permute-start.14 = (bf16[128,256]{1,0:T(8,128)(2,1)S(1)}, bf16[128,256]{1,0:T(8,128)(2,1)S(1)}, u32[]{:S(2)}, u32[]{:S(2)}) collective-permute-start(bf16[128,256]{1,0:T(8,128)(2,1)S(1)} %get-tuple-element.22), channel_id=1, source_target_pairs={{0,64},{1,128},{2,192},{3,0},{64,65},{65,129},{66,193},{67,1},{128... | collective-permute-start | bytes 196616 | tf_op jit(solution)/shard_map/ppermute | solution.py:314
  (7 other events, 5.6 us)

commit v4 on v3

v4 whole, which is shorter than its diff:
```python
import math

import jax
import jax.numpy as jnp
from jax import lax
from jax.experimental import pallas as pl
from jax.experimental.pallas import tpu as pltpu
from jax.sharding import Mesh, PartitionSpec as P

HEADS = 128
KV_HEADS = 8
HEAD_DIM = 128
GROUP = HEADS // KV_HEADS
HIDE = -1e30
SCALE = 1.0 / math.sqrt(HEAD_DIM)
LOG2E = 1.4426950408889634

X, ZQ, ZP, YL, YH, CORE = 4, 4, 2, 2, 2, 2
NEAR = ZP * YL
MEMBERS = ZQ * NEAR
CTX_AXES = ("x", "zq", "zp", "yl")
TP_AXES = ("yh", "c")
NEAR_AXES = ("zp", "yl")
ZY_AXES = ("zq", "zp", "yl")
TOK = 8
ROWS = 512
SPAN = 16
GTOK = MEMBERS * TOK
GATHERED = ZQ * TOK
KV_LOCAL = 2
HEADS_LOCAL = KV_LOCAL * GROUP
WIDTH = HEADS_LOCAL * HEAD_DIM
PARTS = X
STRIDE = ROWS + SPAN
COLS = 2176
STEPS = (0, 1, 3, 2)


def step_of(k):
    return jnp.where(k == 2, 3, jnp.where(k == 3, 2, k))


def collect_kernel(cache_k, cache_v, span_k, span_v, own, sems):
    copies = []
    for side, cache in enumerate((cache_k, cache_v)):
        for g in range(KV_LOCAL):
            copies.append(
                pltpu.make_async_copy(
                    cache.at[:, pl.ds(g * 128, 128)],
                    own.at[pl.ds(g * (ROWS + SPAN), ROWS), pl.ds(side * 128, 128)],
                    sems.at[side * KV_LOCAL + g],
                )
            )
    for copy in copies:
        copy.start()
    empty = jnp.zeros((TOK, 256), jnp.float32)
    for side, span in enumerate((span_k, span_v)):
        padded = jnp.concatenate([span[...].astype(jnp.float32), empty], axis=0)
        padded = padded.astype(jnp.bfloat16)
        for g in range(KV_LOCAL):
            at = g * (ROWS + SPAN) + ROWS
            own[at : at + SPAN, side * 128 : side * 128 + 128] = padded[:, g * 128 : g * 128 + 128]
    for copy in copies:
        copy.wait()


def collect(cache_keys, cache_values, span_keys, span_values):
    vmem, either = pl.BlockSpec(memory_space=pltpu.VMEM), pl.BlockSpec(memory_space=pl.ANY)
    return pl.pallas_call(
        collect_kernel,
        out_shape=pltpu.HBM((KV_LOCAL * (ROWS + SPAN), 256), jnp.bfloat16),
        in_specs=[either, either, vmem, vmem],
        out_specs=vmem,
        scratch_shapes=[pltpu.SemaphoreType.DMA((2 * KV_LOCAL,))],
        compiler_params=pltpu.CompilerParams(vmem_limit_bytes=4 << 20),
        cost_estimate=pl.CostEstimate(flops=1 << 16, bytes_accessed=1 << 20, transcendentals=0),
        name="collect",
    )(cache_keys, cache_values, span_keys, span_values)


def pack_kernel(queries, size0, size1, size2, size3, message):
    lane = lax.broadcasted_iota(jnp.int32, (TOK, 128), 1)
    tail = jnp.zeros((TOK, 128), jnp.int32)
    for k, size in enumerate((size0, size1, size2, size3)):
        high = size[0] // 256
        tail = jnp.where(lane == k, high, tail)
        tail = jnp.where(lane == PARTS + k, size[0] - high * 256, tail)
    message[:, 0:WIDTH] = queries[...]
    message[:, WIDTH : WIDTH + 128] = tail.astype(jnp.float32).astype(jnp.bfloat16)


def pack(queries, sizes):
    vmem = pl.BlockSpec(memory_space=pltpu.VMEM)
    return pl.pallas_call(
        pack_kernel,
        out_shape=jax.ShapeDtypeStruct((TOK, WIDTH + 128), jnp.bfloat16),
        in_specs=[vmem] + [pl.BlockSpec(memory_space=pltpu.SMEM)] * PARTS,
        out_specs=vmem,
        compiler_params=pltpu.CompilerParams(vmem_limit_bytes=2 << 20),
        cost_estimate=pl.CostEstimate(flops=1 << 16, bytes_accessed=1 << 17, transcendentals=0),
        name="pack",
    )(queries, *sizes)


def places(zq, near):
    return [((zq + b) % ZQ) * NEAR + (near + c) % NEAR for c in range(NEAR) for b in range(ZQ)]


def place_of(rows, zq, near):
    return ((zq + (rows // TOK) % ZQ) % ZQ) * NEAR + (near + rows // GATHERED) % NEAR


def visible_rows(info, tail):
    lane = lax.broadcasted_iota(jnp.int32, (GTOK, 128), 1)
    row = lax.broadcasted_iota(jnp.int32, (GTOK, 128), 0)
    held = (row % TOK == 0) & (lane < 2 * PARTS)
    size = jnp.where(held, tail * jnp.where(lane < PARTS, 256.0, 1.0), 0.0)
    x = (info[1] + step_of(lane % PARTS)) % X
    shard = x * MEMBERS + place_of(row, info[2], info[3])
    start = info[0].astype(jnp.float32)
    out = []
    for k in range(PARTS):
        own = ((info[1] + STEPS[k]) % X) * MEMBERS + info[2] * NEAR + info[3]
        offset = jnp.sum(jnp.where(shard < own, size, 0.0), keepdims=True)
        filled = jnp.sum(jnp.where(shard == own, size, 0.0), keepdims=True)
        out.append(jnp.clip(start - offset, 0.0, filled))
    return out


def attend_kernel(info, *refs):
    q_hbm, (own, following, previous, far0, far1) = refs[:NEAR], refs[NEAR : NEAR + 5]
    out_hbm, keys, values, seen, q_ref, res_ref, stat_ref, out_ref = refs[NEAR + 5 : NEAR + 13]
    kv_sems, q_sems, out_sems = refs[NEAR + 13 :]
    half = WIDTH // KV_LOCAL
    spans = [pl.ds(g * half, half) for g in range(KV_LOCAL)] + [pl.ds(WIDTH, 128)]

    def fetches(i):
        return [
            pltpu.make_async_copy(
                q_hbm[c].at[:, spans[i]],
                q_ref.at[pl.ds(c * GATHERED, GATHERED), spans[i]],
                q_sems.at[i * NEAR + c],
            )
            for c in range(NEAR)
        ]

    def loads(g):
        copies = []
        for k, kv in enumerate((own, following, previous, (far0, far1)[g])):
            first = 0 if k == PARTS - 1 else g * STRIDE
            for side, to in enumerate((keys, values)):
                copies.append(
                    pltpu.make_async_copy(
                        kv.at[pl.ds(first, STRIDE), pl.ds(side * 128, 128)],
                        to.at[g, pl.ds(k * STRIDE, STRIDE), pl.ds(0, 128)],
                        kv_sems.at[(g * PARTS + k) * 2 + side],
                    )
                )
        return copies

    def store(i):
        return pltpu.make_async_copy(
            out_ref.at[:, spans[i]], out_hbm.at[:, spans[i]], out_sems.at[i]
        )

    for copy in fetches(KV_LOCAL):
        copy.start()
    for g in range(KV_LOCAL):
        for copy in fetches(g) + loads(g):
            copy.start()
    lane = lax.broadcasted_iota(jnp.int32, (128, 128), 1)
    row = lax.broadcasted_iota(jnp.int32, (128, 128), 0)
    spare = COLS - PARTS * STRIDE
    for g in range(KV_LOCAL):
        at = pl.ds(PARTS * STRIDE, spare)
        keys[g, at, 0:128] = jnp.zeros((spare, 128), jnp.bfloat16)
        keys[g, at, 128:256] = jnp.where(lane == 0, HIDE, 0.0)[:spare].astype(jnp.bfloat16)
        values[g, at, 0:128] = jnp.zeros((spare, 128), jnp.bfloat16)
        values[g, :, 128:256] = jnp.ones((COLS, 128), jnp.bfloat16)
    slot = lane - 64
    part, inner = slot // SPAN, slot % SPAN
    shard = ((info[1] + step_of(part)) % X) * MEMBERS + info[2] * NEAR + info[3]
    token = (info[1] * MEMBERS + place_of(row, info[2], info[3])) * TOK + row % TOK
    hidden = (inner >= TOK) | (shard * TOK + inner > token)
    extra = jnp.where(lane == 0, 1.0, jnp.where((slot >= 0) & hidden, HIDE, 0.0))
    seen[...] = extra.astype(jnp.bfloat16)
    for copy in fetches(KV_LOCAL):
        copy.wait()
    limits = visible_rows(info, q_ref[:, WIDTH : WIDTH + 128].astype(jnp.float32))
    lane = lax.broadcasted_iota(jnp.int32, (STRIDE, 128), 1)
    row = lax.broadcasted_iota(jnp.int32, (STRIDE, 128), 0)
    for k in range(PARTS):
        cached = (lane == 0) & (row < ROWS) & (row.astype(jnp.float32) >= limits[k])
        mark = (row >= ROWS) & (lane == 64 + k * SPAN + row - ROWS)
        bias = jnp.where(cached, HIDE, jnp.where(mark, 1.0, 0.0)).astype(jnp.bfloat16)
        for g in range(KV_LOCAL):
            keys[g, pl.ds(k * STRIDE, STRIDE), 128:256] = bias

    order = places(info[2], info[3])

    def arrange(ref, at, block):
        for piece, place in enumerate(order):
            to = pl.ds(pl.multiple_of(place * TOK, TOK), TOK)
            ref[to, at] = block[piece * TOK : (piece + 1) * TOK]

    per = 2
    lane = lax.broadcasted_iota(jnp.int32, (GTOK, 128), 1)
    mask = jnp.concatenate([seen[...]] * per, axis=0)
    stats = jnp.zeros((GTOK, 128), jnp.float32)
    for g in range(KV_LOCAL):
        for copy in fetches(g) + loads(g):
            copy.wait()

        def columns(h):
            return pl.ds((g * GROUP + h) * 128, 128)

        def score(i):
            heads = [q_ref[:, columns(i * per + j)] for j in range(per)]
            query = jnp.concatenate([jnp.concatenate(heads, axis=0), mask], axis=1)
            return lax.dot_general(
                query, keys[g], (((1,), (1,)), ((), ())), preferred_element_type=jnp.float32
            )

        scores = score(0)
        for i in range(GROUP // per):
            later = score(i + 1) if i + 1 < GROUP // per else None
            top = jnp.max(scores, axis=1, keepdims=True)
            weights = jnp.exp2((scores - top) * (SCALE * LOG2E)).astype(jnp.bfloat16)
            both = jnp.dot(weights, values[g], preferred_element_type=jnp.float32)
            total = both[:, 128:256]
            outs = both[:, 0:128] / total
            lse = top * SCALE + jnp.log(total)
            for j in range(per):
                h = i * per + j
                arrange(res_ref, columns(h), outs[j * GTOK : (j + 1) * GTOK])
                mine = lane % HEADS_LOCAL == g * GROUP + h
                stats = jnp.where(mine, lse[j * GTOK : (j + 1) * GTOK], stats)
            scores = later
        out_ref[:, spans[g]] = res_ref[:, spans[g]].astype(jnp.bfloat16)
        store(g).start()
    arrange(stat_ref, pl.ds(0, 128), stats)
    stats = stat_ref[...]
    high = stats.astype(jnp.bfloat16).astype(jnp.float32)
    rest = stats - high
    middle = rest.astype(jnp.bfloat16).astype(jnp.float32)
    low = rest - middle
    pieces = jnp.where(lane < HEADS_LOCAL, high, jnp.where(lane < 2 * HEADS_LOCAL, middle, low))
    out_ref[:, WIDTH : WIDTH + 128] = pieces.astype(jnp.bfloat16)
    store(KV_LOCAL).start()
    for i in range(KV_LOCAL + 1):
        store(i).wait()


def attend(info, queries, parts):
    hbm = pl.BlockSpec(memory_space=pltpu.HBM)
    operands = [pltpu.with_memory_space_constraint(v, pltpu.HBM) for v in (*queries, *parts)]
    return pl.pallas_call(
        attend_kernel,
        out_shape=pltpu.HBM((GTOK, WIDTH + 128), jnp.bfloat16),
        in_specs=[pl.BlockSpec(memory_space=pltpu.SMEM)] + [hbm] * len(operands),
        out_specs=hbm,
        scratch_shapes=[
            pltpu.VMEM((KV_LOCAL, COLS, 256), jnp.bfloat16),
            pltpu.VMEM((KV_LOCAL, COLS, 256), jnp.bfloat16),
            pltpu.VMEM((GTOK, 128), jnp.bfloat16),
            pltpu.VMEM((GTOK, WIDTH + 128), jnp.bfloat16),
            pltpu.VMEM((GTOK, WIDTH), jnp.float32),
            pltpu.VMEM((GTOK, 128), jnp.float32),
            pltpu.VMEM((GTOK, WIDTH + 128), jnp.bfloat16),
            pltpu.SemaphoreType.DMA((2 * KV_LOCAL * PARTS,)),
            pltpu.SemaphoreType.DMA(((KV_LOCAL + 1) * NEAR,)),
            pltpu.SemaphoreType.DMA((KV_LOCAL + 1,)),
        ],
        compiler_params=pltpu.CompilerParams(vmem_limit_bytes=24 << 20),
        cost_estimate=pl.CostEstimate(
            flops=8 * HEADS_LOCAL * GTOK * COLS * 128,
            bytes_accessed=4 << 20,
            transcendentals=HEADS_LOCAL * GTOK * COLS,
        ),
        name="attend",
    )(info, *operands)


def merge_kernel(got, out_ref):
    pieces = got[:, :, WIDTH : WIDTH + 128].astype(jnp.float32)
    lse = pieces + (pltpu.roll(pieces, 96, 2) + pltpu.roll(pieces, 64, 2))
    share = jnp.exp(lse - jnp.max(lse, axis=0, keepdims=True))
    share = share / jnp.sum(share, axis=0, keepdims=True)
    for h in range(HEADS_LOCAL):
        at = slice(h * 128, (h + 1) * 128)
        merged = jnp.sum(share[:, :, h : h + 1] * got[:, :, at].astype(jnp.float32), axis=0)
        out_ref[:, at] = merged.astype(jnp.bfloat16)


def merge(got):
    vmem = pl.BlockSpec(memory_space=pltpu.VMEM)
    return pl.pallas_call(
        merge_kernel,
        out_shape=jax.ShapeDtypeStruct((TOK, WIDTH), jnp.bfloat16),
        in_specs=[vmem],
        out_specs=vmem,
        compiler_params=pltpu.CompilerParams(vmem_limit_bytes=6 << 20),
        cost_estimate=pl.CostEstimate(flops=2 << 20, bytes_accessed=1 << 20, transcendentals=4096),
        name="merge",
    )(got)


def project_kernel(info, *refs):
    gathered, pieces, (out_ref, rows_ref) = refs[:NEAR], iter(refs[NEAR:-2]), refs[-2:]
    order = places(info[2], info[3])
    merged = jnp.concatenate([ref[...] for ref in gathered], axis=0)
    for k in range(X):
        total, at = None, 0
        while at < WIDTH:
            w = next(pieces)
            rows = w.shape[0]
            term = jnp.dot(merged[:, at : at + rows], w[...], preferred_element_type=jnp.float32)
            total = term if total is None else total + term
            at += rows
        for piece, place in enumerate(order):
            to = pl.ds(pl.multiple_of(place * TOK, TOK), TOK)
            rows_ref[k, to, :] = total[piece * TOK : (piece + 1) * TOK]
        out_ref[(k + info[0] - info[1] + X) % X] = rows_ref[k].astype(jnp.bfloat16)


def project(info, gathered, weights):
    vmem = pl.BlockSpec(memory_space=pltpu.VMEM)
    operands = list(gathered) + [w for part in weights for w in part]
    return pl.pallas_call(
        project_kernel,
        out_shape=jax.ShapeDtypeStruct((X, GTOK, 256), jnp.bfloat16),
        in_specs=[pl.BlockSpec(memory_space=pltpu.SMEM)] + [vmem] * len(operands),
        out_specs=vmem,
        scratch_shapes=[pltpu.VMEM((X, GTOK, 256), jnp.float32)],
        compiler_params=pltpu.CompilerParams(vmem_limit_bytes=14 << 20),
        cost_estimate=pl.CostEstimate(
            flops=2 * GTOK * WIDTH * 256 * X, bytes_accessed=10 << 20, transcendentals=0
        ),
        name="project",
    )(info, *operands)


def along(v, axis, k):
    return lax.ppermute(v, axis, [((i + k) % 4, i) for i in range(4)])


def gather(v):
    some = jnp.concatenate([v] + [along(v, "zq", b) for b in range(1, ZQ)], axis=0)
    return [some] + [along(some, NEAR_AXES, c) for c in range(1, NEAR)]


def after(v, *earlier):
    return lax.optimization_barrier((v, *earlier))[0]


def shards(queries, span_keys, span_values, cache_keys, cache_values, lengths, start_pos, w_out):
    x, zq, near = lax.axis_index("x"), lax.axis_index("zq"), lax.axis_index(NEAR_AXES)
    tp = lax.axis_index(TP_AXES)
    info = jnp.stack([start_pos[0], x, zq, near]).astype(jnp.int32)

    own = collect(cache_keys, cache_values, span_keys, span_values)
    following, previous = along(own, "x", 1), along(own, "x", 3)
    far0 = along(following[: ROWS + SPAN], "x", 1)
    far1 = along(previous[ROWS + SPAN :], "x", 3)

    sizes = [lengths] + [along(lengths, "x", k) for k in STEPS[1:]]
    asked = gather(pack(queries, sizes))

    partial = attend(info, asked, [own, following, previous, far0, far1])
    got = lax.all_to_all(partial.reshape(MEMBERS, TOK, WIDTH + 128), ZY_AXES, 0, 0, tiled=True)

    half = WIDTH // 2
    own_a, own_b = w_out[:half], w_out[half:]
    next_a = along(after(own_a, far0, far1), "x", 1)
    last_b = along(after(own_b, far0, far1), "x", 3)
    far_a = along(after(next_a, last_b), "x", 1)
    far_b = along(after(last_b, next_a), "x", 3)
    next_b = along(after(own_b, far_a, far_b), "x", 1)
    last_a = along(after(own_a, far_a, far_b), "x", 3)
    weights = [(own_a, own_b), (next_a, next_b), (far_a, far_b), (last_a, last_b)]

    attention = gather(after(merge(got), far_a, far_b))

    info = jnp.stack([x, tp, zq, near]).astype(jnp.int32)
    projected = project(info, attention, weights)
    total = None
    for r in range(X):
        pairs = [(a * 4 + b, ((b + r) % X) * 4 + a) for a in range(X) for b in range(4)]
        term = lax.ppermute(projected[r], ("x", "yh", "c"), pairs).astype(jnp.float32)
        total = term if total is None else total + term
    return total.astype(jnp.bfloat16)


def solution(mesh):
    fine = Mesh(mesh.devices.reshape(X, ZQ, ZP, YL, YH, CORE), CTX_AXES + TP_AXES)
    split = P(CTX_AXES, TP_AXES)
    return jax.shard_map(
        shards,
        mesh=fine,
        in_specs=(split, split, split, split, split, P(CTX_AXES), P(), P(TP_AXES, CTX_AXES)),
        out_specs=P(TP_AXES, CTX_AXES),
        check_vma=False,
    )
```

time: 153 us -> 142 us (0.928)
  waiting for transfers between devices: 69.3 us -> 53.5 us
  starting transfers between devices: 46.3 us -> 57.4 us
  local copies, waits for them, and re-layouts: 11.1 us -> 5.12 us
    ppermute x13 -> x25, starting transfers between devices: 15.7 us -> 45.3 us  [along(): return lax.ppermute(v, axis, [((i + k) % 4, i) for i in range(4)])]
    all_to_all x2 -> x0, starting transfers between devices: 13.3 us -> none  [the longest x1 9.44 us: shards(): lax.all_to_all(packed, ZY_AXES, 0, 0, tiled=True).reshape(GTOK, WIDTH + 128)]
    ppermute x13 -> x25, waiting for transfers between devices: 38.4 us -> 28.9 us  [along(): return lax.ppermute(v, axis, [((i + k) % 4, i) for i in range(4)])]
    unnamed x22 -> x21, local copies, waits for them, and re-layouts: 9.41 us -> 4.92 us
    all_to_all x2 -> x0, waiting for transfers between devices: 4.37 us -> none  [the longest x1 3.03 us: shards(): lax.all_to_all(packed, ZY_AXES, 0, 0, tiled=True).reshape(GTOK, WIDTH + 128)]
    all_to_all x1, waiting for transfers between devices: 22.1 us -> 17.8 us  [shards(): lax.all_to_all(partial.reshape(MEMBERS, TOK, WIDTH + 128), ZY_AXES, 0, 0,...]
    all_to_all x1, starting transfers between devices: 7.44 us -> 3.71 us  [shards(): lax.all_to_all(partial.reshape(MEMBERS, TOK, WIDTH + 128), ZY_AXES, 0, 0,...]
    ppermute x4, waiting for transfers between devices: 4.39 us -> 6.77 us  [shards(): lax.ppermute(projected[r], ('x', 'yh', 'c'), pairs).astype(jnp.float32)]
  transfers between devices with their start and end apart: 20 -> 30, of which waited for: 10 -> 15; matrix products, arithmetic and copies ran while one was open for 1% -> 0% of each run, Pallas kernels for 10% -> 12%
where the time goes in v4:
time: 142 us; the launch traced here: 141 us
  starting transfers between devices  57.4 us (40%)
  waiting for transfers between devices  53.5 us (38%)
  Pallas kernels  22.9 us (16%)
  local copies, waits for them, and re-layouts  5.12 us (4%)
  between operations  1.54 us (1%)
    ppermute x25, starting transfers between devices, along(): return lax.ppermute(v, axis, [((i + k) % 4, i) for i in range(4)])  45.3 us
    ppermute x25, waiting for transfers between devices, along(): return lax.ppermute(v, axis, [((i + k) % 4, i) for i in range(4)])  28.9 us
    all_to_all x1, waiting for transfers between devices, shards(): lax.all_to_all(partial.reshape(MEMBERS, TOK, WIDTH + 128), ZY_AXES, 0, 0,...  17.8 us
    pallas_call x1, Pallas kernels, attend(): pl.pallas_call(attend_kernel, out_shape=pltpu.HBM((GTOK, WIDTH + 128), jn...  15.3 us
    ppermute x4, starting transfers between devices, shards(): lax.ppermute(projected[r], ('x', 'yh', 'c'), pairs).astype(jnp.float32)  8.43 us
    ppermute x4, waiting for transfers between devices, shards(): lax.ppermute(projected[r], ('x', 'yh', 'c'), pairs).astype(jnp.float32)  6.77 us
    unnamed x21, local copies, waits for them, and re-layouts  4.92 us
    pallas_call x1, Pallas kernels, project(): pl.pallas_call(project_kernel, out_shape=jax.ShapeDtypeStruct((X, GTOK, 2...  4.02 us
  transfers between devices with their start and end apart: 30, of which 15 were waited for; matrix products, arithmetic and copies ran while one was open for 0% of the time, Pallas kernels for 12%

profile of v4, /device:TPU:2, one launch (start us, length us, event | category | flops | bytes accessed | tf_op | source)
XLA Modules:
  0.0 141.3 jit_solution(9678240100698701986)
XLA Ops:
  2.3 2.1 %collective-permute-start.2 = (s32[1]{0:T(128)}, s32[1]{0:T(128)}, u32[]{:S(2)}, u32[]{:S(2)}) collective-permute-start(s32[1]{0:T(128)} %param.13), channel_id=1, source_target_pairs={{128,0},{192,64},{0,128},{64,192},{129,1},{193,65},{1,129},{65,193... | collective-permute-start | bytes 20 | tf_op jit(solution)/shard_map/ppermute | solution.py:344
  5.3 2.1 %collective-permute-done.2.size3 = s32[1]{0:T(128)} collective-permute-done((s32[1]{0:T(128)}, s32[1]{0:T(128)}, u32[]{:S(2)}, u32[]{:S(2)}) %collective-permute-start.2) | collective-permute-done | bytes 36 | tf_op jit(solution)/shard_map/ppermute | solution.py:344
  10.1 3.1 %collective-permute-start.5 = (bf16[8,4224]{1,0:T(8,128)(2,1)S(1)}, bf16[8,4224]{1,0:T(8,128)(2,1)S(1)}, u32[]{:S(2)}, u32[]{:S(2)}) collective-permute-start(bf16[8,4224]{1,0:T(8,128)(2,1)S(1)} %pack.1), channel_id=1, source_target_pairs={{48,0},{0,16},{16,32},{32,48},{49,1},{1,17},{17,33},{33,49},{50,2}... | collective-permute-start | bytes 202760 | tf_op jit(solution)/shard_map/ppermute | solution.py:344
  13.2 5.4 %collective-permute-start.4 = (bf16[8,4224]{1,0:T(8,128)(2,1)S(1)}, bf16[8,4224]{1,0:T(8,128)(2,1)S(1)}, u32[]{:S(2)}, u32[]{:S(2)}) collective-permute-start(bf16[8,4224]{1,0:T(8,128)(2,1)S(1)} %pack.1), channel_id=1, source_target_pairs={{32,0},{48,16},{0,32},{16,48},{33,1},{49,17},{1,33},{17,49},{34,2}... | collective-permute-start | bytes 202760 | tf_op jit(solution)/shard_map/ppermute | solution.py:344
  18.6 2.7 %collective-permute-start.3 = (bf16[8,4224]{1,0:T(8,128)(2,1)S(1)}, bf16[8,4224]{1,0:T(8,128)(2,1)S(1)}, u32[]{:S(2)}, u32[]{:S(2)}) collective-permute-start(bf16[8,4224]{1,0:T(8,128)(2,1)S(1)} %pack.1), channel_id=1, source_target_pairs={{16,0},{32,16},{48,32},{0,48},{17,1},{33,17},{49,33},{1,49},{18,2}... | collective-permute-start | bytes 202760 | tf_op jit(solution)/shard_map/ppermute | solution.py:344
  31.7 5.7 %collective-permute-done.10.refs_6_ = bf16[1056,256]{1,0:T(8,128)(2,1)S(1)} collective-permute-done((bf16[1056,256]{1,0:T(8,128)(2,1)}, bf16[1056,256]{1,0:T(8,128)(2,1)S(1)}, u32[]{:S(2)}, u32[]{:S(2)}) %collective-permute-start.10) | collective-permute-done | bytes 540704 | tf_op jit(solution)/shard_map/ppermute | solution.py:344
  37.4 2.2 %collective-permute-start.12 = (bf16[528,256]{1,0:T(8,128)(2,1)S(1)}, bf16[528,256]{1,0:T(8,128)(2,1)}, u32[]{:S(2)}, u32[]{:S(2)}) collective-permute-start(bf16[528,256]{1,0:T(8,128)(2,1)S(1)} %slice.33), channel_id=1, source_target_pairs={{192,0},{0,64},{64,128},{128,192},{193,1},{1,65},{65,129},{129,193... | collective-permute-start | bytes 811016 | tf_op jit(solution)/shard_map/ppermute | solution.py:344
  42.2 2.8 %collective-permute-done.12.refs_8_ = bf16[528,256]{1,0:T(8,128)(2,1)} collective-permute-done((bf16[528,256]{1,0:T(8,128)(2,1)S(1)}, bf16[528,256]{1,0:T(8,128)(2,1)}, u32[]{:S(2)}, u32[]{:S(2)}) %collective-permute-start.12) | collective-permute-done | bytes 270368 | tf_op jit(solution)/shard_map/ppermute | solution.py:344
  45.0 3.9 %collective-permute-done.11.refs_7_ = bf16[528,256]{1,0:T(8,128)(2,1)} collective-permute-done((bf16[528,256]{1,0:T(8,128)(2,1)S(1)}, bf16[528,256]{1,0:T(8,128)(2,1)}, u32[]{:S(2)}, u32[]{:S(2)}) %collective-permute-start.11) | collective-permute-done | bytes 270368 | tf_op jit(solution)/shard_map/ppermute | solution.py:344
  50.9 15.3 %attend.1 = bf16[128,4224]{1,0:T(8,128)(2,1)} custom-call(s32[4]{0:T(128)S(1)} %add_add_fusion.1.info, bf16[32,4224]{1,0:T(8,128)(2,1)} %copy-done.6, bf16[32,4224]{1,0:T(8,128)(2,1)} %collective-permute-done.6.refs_1_, bf16[32,4224]{1,0:T(8,128)(2,1)} %collective-permute-done.7.refs_2_, bf16[32,4224]{1,0:T(8,128)(2,1)} %collective-permute-done.8.refs_3_, ...), custom_call_target="tpu_custom_call" | custom-call | flops 9126805504 | bytes 4194304 | tf_op jit(solution)/shard_map/attend/pallas_call | solution.py:257
  66.2 3.7 %all-to-all-start = ((bf16[16,8,4224]{2,1,0:T(8,128)(2,1)}), bf16[16,8,4224]{2,1,0:T(8,128)(2,1)S(1)}, u32[]{:S(2)}, u32[]{:S(2)}) async-start(bf16[16,8,4224]{2,1,0:T(8,128)(2,1)} %bitcast.13), calls=%async_computation | async-start | bytes 2162688 | tf_op jit(solution)/shard_map/all_to_all | solution.py:370
  69.9 2.1 %collective-permute-done.13.refs_6_ = bf16[2048,256]{1,0:T(8,128)(2,1)} collective-permute-done((bf16[2048,256]{1,0:T(8,128)(2,1)S(1)}, bf16[2048,256]{1,0:T(8,128)(2,1)}, u32[]{:S(2)}, u32[]{:S(2)}) %collective-permute-start.13) | collective-permute-done | bytes 1048608 | tf_op jit(solution)/shard_map/ppermute | solution.py:344
  74.0 17.8 %all-to-all-done.got = bf16[16,8,4224]{2,1,0:T(8,128)(2,1)S(1)} async-done(((bf16[16,8,4224]{2,1,0:T(8,128)(2,1)}), bf16[16,8,4224]{2,1,0:T(8,128)(2,1)S(1)}, u32[]{:S(2)}, u32[]{:S(2)}) %all-to-all-start) | async-done | bytes 1081376 | tf_op jit(solution)/shard_map/all_to_all | solution.py:370
  93.0 2.0 %collective-permute-start.19 = (bf16[8,4096]{1,0:T(8,128)(2,1)S(1)}, bf16[8,4096]{1,0:T(8,128)(2,1)S(1)}, u32[]{:S(2)}, u32[]{:S(2)}) collective-permute-start(bf16[8,4096]{1,0:T(8,128)(2,1)S(1)} %merge.1), channel_id=1, source_target_pairs={{48,0},{0,16},{16,32},{32,48},{49,1},{1,17},{17,33},{33,49},{50,2}... | collective-permute-start | bytes 196616 | tf_op jit(solution)/shard_map/ppermute | solution.py:344
  95.0 3.6 %collective-permute-start.18 = (bf16[8,4096]{1,0:T(8,128)(2,1)S(1)}, bf16[8,4096]{1,0:T(8,128)(2,1)S(1)}, u32[]{:S(2)}, u32[]{:S(2)}) collective-permute-start(bf16[8,4096]{1,0:T(8,128)(2,1)S(1)} %merge.1), channel_id=1, source_target_pairs={{32,0},{48,16},{0,32},{16,48},{33,1},{49,17},{1,33},{17,49},{34,2}... | collective-permute-start | bytes 196616 | tf_op jit(solution)/shard_map/ppermute | solution.py:344
  98.6 3.6 %collective-permute-start.17 = (bf16[8,4096]{1,0:T(8,128)(2,1)S(1)}, bf16[8,4096]{1,0:T(8,128)(2,1)S(1)}, u32[]{:S(2)}, u32[]{:S(2)}) collective-permute-start(bf16[8,4096]{1,0:T(8,128)(2,1)S(1)} %merge.1), channel_id=1, source_target_pairs={{16,0},{32,16},{48,32},{0,48},{17,1},{33,17},{49,33},{1,49},{18,2}... | collective-permute-start | bytes 196616 | tf_op jit(solution)/shard_map/ppermute | solution.py:344
  102.2 3.0 %collective-permute-start.23 = (bf16[2048,256]{1,0:T(8,128)(2,1)S(1)}, bf16[2048,256]{1,0:T(8,128)(2,1)S(1)}, u32[]{:S(2)}, u32[]{:S(2)}) collective-permute-start(bf16[2048,256]{1,0:T(8,128)(2,1)S(1)} %get-tuple-element.17.refs_5_), channel_id=1, source_target_pairs={{64,0},{128,64},{192,128},{0,192},{65,1},{129,65},{193,129},{1,193... | collective-permute-start | bytes 3145736 | tf_op jit(solution)/shard_map/ppermute | solution.py:344
  109.6 3.1 %collective-permute-done.22.refs_3_ = bf16[32,4096]{1,0:T(8,128)(2,1)} collective-permute-done((bf16[32,4096]{1,0:T(8,128)(2,1)S(1)}, bf16[32,4096]{1,0:T(8,128)(2,1)}, u32[]{:S(2)}, u32[]{:S(2)}) %collective-permute-start.22) | collective-permute-done | bytes 262176 | tf_op jit(solution)/shard_map/ppermute | solution.py:344
  113.2 2.2 %collective-permute-done.20.refs_1_ = bf16[32,4096]{1,0:T(8,128)(2,1)} collective-permute-done((bf16[32,4096]{1,0:T(8,128)(2,1)S(1)}, bf16[32,4096]{1,0:T(8,128)(2,1)}, u32[]{:S(2)}, u32[]{:S(2)}) %collective-permute-start.20) | collective-permute-done | bytes 262176 | tf_op jit(solution)/shard_map/ppermute | solution.py:344
  115.4 3.6 %collective-permute-done.23.refs_7_ = bf16[2048,256]{1,0:T(8,128)(2,1)S(1)} collective-permute-done((bf16[2048,256]{1,0:T(8,128)(2,1)S(1)}, bf16[2048,256]{1,0:T(8,128)(2,1)S(1)}, u32[]{:S(2)}, u32[]{:S(2)}) %collective-permute-start.23) | collective-permute-done | bytes 1048608 | tf_op jit(solution)/shard_map/ppermute | solution.py:344
  119.0 2.3 %collective-permute-done.24.refs_10_ = bf16[2048,256]{1,0:T(8,128)(2,1)} collective-permute-done((bf16[2048,256]{1,0:T(8,128)(2,1)S(1)}, bf16[2048,256]{1,0:T(8,128)(2,1)}, u32[]{:S(2)}, u32[]{:S(2)}) %collective-permute-start.24) | collective-permute-done | bytes 1048608 | tf_op jit(solution)/shard_map/ppermute | solution.py:344
  121.3 4.0 %project.1 = bf16[4,128,256]{2,1,0:T(8,128)(2,1)S(1)} custom-call(s32[4]{0:T(128)S(1)} %add_add_fusion.info, bf16[32,4096]{1,0:T(8,128)(2,1)S(1)} %constant_dynamic-update-slice_fusion.refs_0_, bf16[32,4096]{1,0:T(8,128)(2,1)} %collective-permute-done.20.refs_1_, bf16[32,4096]{1,0:T(8,128)(2,1)} %collective-permute-done.21.refs_2_, ...), custom_call_target="tpu_custom_call" | custom-call | flops 1073741824 | bytes 10485760 | tf_op jit(solution)/shard_map/project/pallas_call | solution.py:329
  127.4 6.1 %collective-permute-start.27 = (bf16[128,256]{1,0:T(8,128)(2,1)S(1)}, bf16[128,256]{1,0:T(8,128)(2,1)S(1)}, u32[]{:S(2)}, u32[]{:S(2)}) collective-permute-start(bf16[128,256]{1,0:T(8,128)(2,1)S(1)} %get-tuple-element.23), channel_id=1, source_target_pairs={{0,128},{1,192},{2,0},{3,64},{64,129},{65,193},{66,1},{67,65},{128... | collective-permute-start | bytes 196616 | tf_op jit(solution)/shard_map/ppermute | solution.py:389
  135.1 5.5 %collective-permute-done.27 = bf16[128,256]{1,0:T(8,128)(2,1)S(1)} collective-permute-done((bf16[128,256]{1,0:T(8,128)(2,1)S(1)}, bf16[128,256]{1,0:T(8,128)(2,1)S(1)}, u32[]{:S(2)}, u32[]{:S(2)}) %collective-permute-start.27) | collective-permute-done | bytes 65568 | tf_op jit(solution)/shard_map/ppermute | solution.py:389
  (71 shorter events, 32.0 us)
Async XLA Ops:
  10.1 17.5 %collective-permute-start.5 = (bf16[8,4224]{1,0:T(8,128)(2,1)S(1)}, bf16[8,4224]{1,0:T(8,128)(2,1)S(1)}, u32[]{:S(2)}, u32[]{:S(2)}) collective-permute-start(bf16[8,4224]{1,0:T(8,128)(2,1)S(1)} %pack.1), channel_id=1, source_target_pairs={{48,0},{0,16},{16,32},{32,48},{49,1},{1,17},{17,33},{33,49},{50,2}... | collective-permute-start | bytes 202760 | tf_op jit(solution)/shard_map/ppermute | solution.py:344
  13.2 14.4 %collective-permute-start.4 = (bf16[8,4224]{1,0:T(8,128)(2,1)S(1)}, bf16[8,4224]{1,0:T(8,128)(2,1)S(1)}, u32[]{:S(2)}, u32[]{:S(2)}) collective-permute-start(bf16[8,4224]{1,0:T(8,128)(2,1)S(1)} %pack.1), channel_id=1, source_target_pairs={{32,0},{48,16},{0,32},{16,48},{33,1},{49,17},{1,33},{17,49},{34,2}... | collective-permute-start | bytes 202760 | tf_op jit(solution)/shard_map/ppermute | solution.py:344
  18.6 9.0 %collective-permute-start.3 = (bf16[8,4224]{1,0:T(8,128)(2,1)S(1)}, bf16[8,4224]{1,0:T(8,128)(2,1)S(1)}, u32[]{:S(2)}, u32[]{:S(2)}) collective-permute-start(bf16[8,4224]{1,0:T(8,128)(2,1)S(1)} %pack.1), channel_id=1, source_target_pairs={{16,0},{32,16},{48,32},{0,48},{17,1},{33,17},{49,33},{1,49},{18,2}... | collective-permute-start | bytes 202760 | tf_op jit(solution)/shard_map/ppermute | solution.py:344
  25.5 11.9 %collective-permute-start.10 = (bf16[1056,256]{1,0:T(8,128)(2,1)}, bf16[1056,256]{1,0:T(8,128)(2,1)S(1)}, u32[]{:S(2)}, u32[]{:S(2)}) collective-permute-start(bf16[1056,256]{1,0:T(8,128)(2,1)} %collect.1.refs_4_), channel_id=1, source_target_pairs={{192,0},{0,64},{64,128},{128,192},{193,1},{1,65},{65,129},{129,193... | collective-permute-start | bytes 1622024 | tf_op jit(solution)/shard_map/ppermute | solution.py:344
  27.1 12.5 %collective-permute-start.9 = (bf16[1056,256]{1,0:T(8,128)(2,1)}, bf16[1056,256]{1,0:T(8,128)(2,1)S(1)}, u32[]{:S(2)}, u32[]{:S(2)}) collective-permute-start(bf16[1056,256]{1,0:T(8,128)(2,1)} %collect.1.refs_4_), channel_id=1, source_target_pairs={{64,0},{128,64},{192,128},{0,192},{65,1},{129,65},{193,129},{1,193... | collective-permute-start | bytes 1622024 | tf_op jit(solution)/shard_map/ppermute | solution.py:344
  27.6 23.3 %collective-permute-start.8 = (bf16[32,4224]{1,0:T(8,128)(2,1)S(1)}, bf16[32,4224]{1,0:T(8,128)(2,1)}, u32[]{:S(2)}, u32[]{:S(2)}) collective-permute-start(bf16[32,4224]{1,0:T(8,128)(2,1)S(1)} %pad_maximum_fusion.refs_0_), channel_id=1, source_target_pairs={{12,0},{0,4},{4,8},{8,12},{13,1},{1,5},{5,9},{9,13},{14,2},{2,6},{... | collective-permute-start | bytes 811016 | tf_op jit(solution)/shard_map/ppermute | solution.py:344
  29.3 21.6 %collective-permute-start.7 = (bf16[32,4224]{1,0:T(8,128)(2,1)S(1)}, bf16[32,4224]{1,0:T(8,128)(2,1)}, u32[]{:S(2)}, u32[]{:S(2)}) collective-permute-start(bf16[32,4224]{1,0:T(8,128)(2,1)S(1)} %pad_maximum_fusion.refs_0_), channel_id=1, source_target_pairs={{8,0},{12,4},{0,8},{4,12},{9,1},{13,5},{1,9},{5,13},{10,2},{14,6},... | collective-permute-start | bytes 811016 | tf_op jit(solution)/shard_map/ppermute | solution.py:344
  30.3 20.6 %collective-permute-start.6 = (bf16[32,4224]{1,0:T(8,128)(2,1)S(1)}, bf16[32,4224]{1,0:T(8,128)(2,1)}, u32[]{:S(2)}, u32[]{:S(2)}) collective-permute-start(bf16[32,4224]{1,0:T(8,128)(2,1)S(1)} %pad_maximum_fusion.refs_0_), channel_id=1, source_target_pairs={{4,0},{8,4},{12,8},{0,12},{5,1},{9,5},{13,9},{1,13},{6,2},{10,6},{... | collective-permute-start | bytes 811016 | tf_op jit(solution)/shard_map/ppermute | solution.py:344
  37.4 7.6 %collective-permute-start.12 = (bf16[528,256]{1,0:T(8,128)(2,1)S(1)}, bf16[528,256]{1,0:T(8,128)(2,1)}, u32[]{:S(2)}, u32[]{:S(2)}) collective-permute-start(bf16[528,256]{1,0:T(8,128)(2,1)S(1)} %slice.33), channel_id=1, source_target_pairs={{192,0},{0,64},{64,128},{128,192},{193,1},{1,65},{65,129},{129,193... | collective-permute-start | bytes 811016 | tf_op jit(solution)/shard_map/ppermute | solution.py:344
  40.4 8.5 %collective-permute-start.11 = (bf16[528,256]{1,0:T(8,128)(2,1)S(1)}, bf16[528,256]{1,0:T(8,128)(2,1)}, u32[]{:S(2)}, u32[]{:S(2)}) collective-permute-start(bf16[528,256]{1,0:T(8,128)(2,1)S(1)} %slice.32), channel_id=1, source_target_pairs={{64,0},{128,64},{192,128},{0,192},{65,1},{129,65},{193,129},{1,193... | collective-permute-start | bytes 811016 | tf_op jit(solution)/shard_map/ppermute | solution.py:344
  48.9 23.1 %collective-permute-start.13 = (bf16[2048,256]{1,0:T(8,128)(2,1)S(1)}, bf16[2048,256]{1,0:T(8,128)(2,1)}, u32[]{:S(2)}, u32[]{:S(2)}) collective-permute-start(bf16[2048,256]{1,0:T(8,128)(2,1)S(1)} %get-tuple-element.18.refs_4_), channel_id=1, source_target_pairs={{64,0},{128,64},{192,128},{0,192},{65,1},{129,65},{193,129},{1,193... | collective-permute-start | bytes 3145736 | tf_op jit(solution)/shard_map/ppermute | solution.py:344
  49.4 22.6 %collective-permute-start.14 = (bf16[2048,256]{1,0:T(8,128)(2,1)S(1)}, bf16[2048,256]{1,0:T(8,128)(2,1)}, u32[]{:S(2)}, u32[]{:S(2)}) collective-permute-start(bf16[2048,256]{1,0:T(8,128)(2,1)S(1)} %get-tuple-element.17.refs_5_), channel_id=1, source_target_pairs={{192,0},{0,64},{64,128},{128,192},{193,1},{1,65},{65,129},{129,193... | collective-permute-start | bytes 3145736 | tf_op jit(solution)/shard_map/ppermute | solution.py:344
  66.2 25.7 %all-to-all-start = ((bf16[16,8,4224]{2,1,0:T(8,128)(2,1)}), bf16[16,8,4224]{2,1,0:T(8,128)(2,1)S(1)}, u32[]{:S(2)}, u32[]{:S(2)}) async-start(bf16[16,8,4224]{2,1,0:T(8,128)(2,1)} %bitcast.13), calls=%async_computation | async-start | bytes 2162688 | tf_op jit(solution)/shard_map/all_to_all | solution.py:370
  72.0 20.6 %collective-permute-start.15 = (bf16[2048,256]{1,0:T(8,128)(2,1)}, bf16[2048,256]{1,0:T(8,128)(2,1)}, u32[]{:S(2)}, u32[]{:S(2)}) collective-permute-start(bf16[2048,256]{1,0:T(8,128)(2,1)} %collective-permute-done.13.refs_6_), channel_id=1, source_target_pairs={{64,0},{128,64},{192,128},{0,192},{65,1},{129,65},{193,129},{1,193... | collective-permute-start | bytes 3145736 | tf_op jit(solution)/shard_map/ppermute | solution.py:344
  73.9 19.1 %collective-permute-start.16 = (bf16[2048,256]{1,0:T(8,128)(2,1)}, bf16[2048,256]{1,0:T(8,128)(2,1)}, u32[]{:S(2)}, u32[]{:S(2)}) collective-permute-start(bf16[2048,256]{1,0:T(8,128)(2,1)} %collective-permute-done.14.refs_11_), channel_id=1, source_target_pairs={{192,0},{0,64},{64,128},{128,192},{193,1},{1,65},{65,129},{129,193... | collective-permute-start | bytes 3145736 | tf_op jit(solution)/shard_map/ppermute | solution.py:344
  93.0 12.2 %collective-permute-start.19 = (bf16[8,4096]{1,0:T(8,128)(2,1)S(1)}, bf16[8,4096]{1,0:T(8,128)(2,1)S(1)}, u32[]{:S(2)}, u32[]{:S(2)}) collective-permute-start(bf16[8,4096]{1,0:T(8,128)(2,1)S(1)} %merge.1), channel_id=1, source_target_pairs={{48,0},{0,16},{16,32},{32,48},{49,1},{1,17},{17,33},{33,49},{50,2}... | collective-permute-start | bytes 196616 | tf_op jit(solution)/shard_map/ppermute | solution.py:344
  95.0 10.1 %collective-permute-start.18 = (bf16[8,4096]{1,0:T(8,128)(2,1)S(1)}, bf16[8,4096]{1,0:T(8,128)(2,1)S(1)}, u32[]{:S(2)}, u32[]{:S(2)}) collective-permute-start(bf16[8,4096]{1,0:T(8,128)(2,1)S(1)} %merge.1), channel_id=1, source_target_pairs={{32,0},{48,16},{0,32},{16,48},{33,1},{49,17},{1,33},{17,49},{34,2}... | collective-permute-start | bytes 196616 | tf_op jit(solution)/shard_map/ppermute | solution.py:344
  102.2 16.9 %collective-permute-start.23 = (bf16[2048,256]{1,0:T(8,128)(2,1)S(1)}, bf16[2048,256]{1,0:T(8,128)(2,1)S(1)}, u32[]{:S(2)}, u32[]{:S(2)}) collective-permute-start(bf16[2048,256]{1,0:T(8,128)(2,1)S(1)} %get-tuple-element.17.refs_5_), channel_id=1, source_target_pairs={{64,0},{128,64},{192,128},{0,192},{65,1},{129,65},{193,129},{1,193... | collective-permute-start | bytes 3145736 | tf_op jit(solution)/shard_map/ppermute | solution.py:344
  105.1 16.2 %collective-permute-start.24 = (bf16[2048,256]{1,0:T(8,128)(2,1)S(1)}, bf16[2048,256]{1,0:T(8,128)(2,1)}, u32[]{:S(2)}, u32[]{:S(2)}) collective-permute-start(bf16[2048,256]{1,0:T(8,128)(2,1)S(1)} %get-tuple-element.18.refs_4_), channel_id=1, source_target_pairs={{192,0},{0,64},{64,128},{128,192},{193,1},{1,65},{65,129},{129,193... | collective-permute-start | bytes 3145736 | tf_op jit(solution)/shard_map/ppermute | solution.py:344
  105.2 7.5 %collective-permute-start.22 = (bf16[32,4096]{1,0:T(8,128)(2,1)S(1)}, bf16[32,4096]{1,0:T(8,128)(2,1)}, u32[]{:S(2)}, u32[]{:S(2)}) collective-permute-start(bf16[32,4096]{1,0:T(8,128)(2,1)S(1)} %constant_dynamic-update-slice_fusion.refs_0_), channel_id=1, source_target_pairs={{12,0},{0,4},{4,8},{8,12},{13,1},{1,5},{5,9},{9,13},{14,2},{2,6},{... | collective-permute-start | bytes 786440 | tf_op jit(solution)/shard_map/ppermute | solution.py:344
  108.1 7.4 %collective-permute-start.20 = (bf16[32,4096]{1,0:T(8,128)(2,1)S(1)}, bf16[32,4096]{1,0:T(8,128)(2,1)}, u32[]{:S(2)}, u32[]{:S(2)}) collective-permute-start(bf16[32,4096]{1,0:T(8,128)(2,1)S(1)} %constant_dynamic-update-slice_fusion.refs_0_), channel_id=1, source_target_pairs={{4,0},{8,4},{12,8},{0,12},{5,1},{9,5},{13,9},{1,13},{6,2},{10,6},{... | collective-permute-start | bytes 786440 | tf_op jit(solution)/shard_map/ppermute | solution.py:344
  125.4 8.4 %collective-permute-start.25 = (bf16[128,256]{1,0:T(8,128)(2,1)S(1)}, bf16[128,256]{1,0:T(8,128)(2,1)S(1)}, u32[]{:S(2)}, u32[]{:S(2)}) collective-permute-start(bf16[128,256]{1,0:T(8,128)(2,1)S(1)} %get-tuple-element.21), channel_id=1, source_target_pairs={{0,0},{1,64},{2,128},{3,192},{64,1},{65,65},{66,129},{67,193},{128... | collective-permute-start | bytes 196616 | tf_op jit(solution)/shard_map/ppermute | solution.py:389
  127.3 7.8 %collective-permute-start.28 = (bf16[128,256]{1,0:T(8,128)(2,1)S(1)}, bf16[128,256]{1,0:T(8,128)(2,1)S(1)}, u32[]{:S(2)}, u32[]{:S(2)}) collective-permute-start(bf16[128,256]{1,0:T(8,128)(2,1)S(1)} %get-tuple-element.22), channel_id=1, source_target_pairs={{0,192},{1,0},{2,64},{3,128},{64,193},{65,1},{66,65},{67,129},{128... | collective-permute-start | bytes 196616 | tf_op jit(solution)/shard_map/ppermute | solution.py:389
  127.4 13.2 %collective-permute-start.27 = (bf16[128,256]{1,0:T(8,128)(2,1)S(1)}, bf16[128,256]{1,0:T(8,128)(2,1)S(1)}, u32[]{:S(2)}, u32[]{:S(2)}) collective-permute-start(bf16[128,256]{1,0:T(8,128)(2,1)S(1)} %get-tuple-element.23), channel_id=1, source_target_pairs={{0,128},{1,192},{2,0},{3,64},{64,129},{65,193},{66,1},{67,65},{128... | collective-permute-start | bytes 196616 | tf_op jit(solution)/shard_map/ppermute | solution.py:389
  (15 other events, 73.7 us)
